TPU v7x, 512 devices: a whole 4x8x8 slice. The times are simulated.
512 devices in a mesh: dp: 8 (over x, core), tensor: 64 (over z, y).
Axes of the slice: x: 4, y: 8, z: 8, core: 2. Of those that a mesh axis runs over, the one named last changes fastest.
Arguments:
- embeddings: bfloat16 [65536, 3584], P('tensor', 'dp'), may hold values from -8 to 8
- pairs: int32 [3072, 2], replicated, may hold values from 0 to 511, as said below
- partner: int32 [65536], P('tensor'), may hold values from 0 to 65535, as said below
Outputs:
- lse_terms: float32 [65536], P('tensor')
- embedding_grad: bfloat16 [65536, 3584], P('tensor', 'dp')
Inputs may be any that keep to these rules, and one draw needn't show every extreme that they name: `pairs`: rows 48 * g to 48 * g + 47 belong to tensor index g, which holds blocks g * 8 to g * 8 + 7. In each of these rows the first block is one of index g's blocks and the second block is held by another tensor index; no two rows of one index name second blocks held by the same index. partner[i] lies in i's block, differs from i, and partner[partner[i]] = i.
All inputs are finite; a program needn't handle non-finite values.
Results may differ from a plain program's by a relative error of at most 0.0036.
Values may be sent and summed in bfloat16 or wider, within the bound.
A program may use at most 128 MiB of HBM per device.

v0:
```python
import math

import jax
import jax.numpy as jnp
from jax import lax
from jax.sharding import PartitionSpec as P

D = 3584
BPD = 8


NEG = -1e30


def merged_lse(values, axis):
    top = jnp.max(values, axis=axis, keepdims=True)
    total = jnp.sum(jnp.exp(values - top), axis=axis, keepdims=True)
    return jnp.squeeze(top + jnp.log(total), axis=axis)


def per_device(embeddings, pairs, partner):
    rows_here, width_dev = embeddings.shape
    groups = lax.axis_size("tensor")
    group_idx = lax.axis_index("tensor")
    block_len = rows_here // BPD
    per_group = pairs.shape[0] // groups
    logit_scale = 2.0 / math.sqrt(D)
    own_blocks = embeddings.reshape(BPD, block_len, width_dev)
    my_pairs = lax.dynamic_slice_in_dim(pairs, group_idx * per_group, per_group, 0)
    row_local = my_pairs[:, 0] - group_idx * BPD
    col_owner = my_pairs[:, 1] // BPD
    owner_pick = (col_owner[:, None] == jnp.arange(groups)[None, :]).astype(jnp.float32)
    everyone = pairs.reshape(groups, per_group, 2)
    naming = everyone[:, :, 1] // BPD == group_idx
    asked_local = everyone[:, :, 1] % BPD
    asked_sel = jnp.sum(
        ((asked_local[:, :, None] == jnp.arange(BPD)[None, None, :]) & naming[:, :, None]).astype(
            jnp.float32
        ),
        axis=1,
    )
    asked_block = jnp.where(
        jnp.any(naming, axis=1), jnp.sum(jnp.where(naming, asked_local, 0), axis=1), BPD
    )
    diag_partial = jnp.einsum(
        "kiw,kjw->kij", own_blocks, own_blocks, preferred_element_type=jnp.float32
    )
    outgoing = jnp.einsum(
        "rb,bnw->rnw",
        asked_sel.astype(jnp.bfloat16),
        own_blocks,
        preferred_element_type=jnp.float32,
    ).astype(jnp.bfloat16)
    fetched = lax.all_to_all(outgoing, "tensor", split_axis=0, concat_axis=0, tiled=True)
    second_rows = jnp.take(fetched, col_owner, axis=0)
    first_rows = jnp.take(own_blocks, row_local, axis=0)
    pair_partial = jnp.einsum(
        "kiw,kjw->kij", first_rows, second_rows, preferred_element_type=jnp.float32
    )
    diag_summed, pair_summed = lax.psum((diag_partial, pair_partial), "dp")
    self_mask = jnp.eye(block_len, dtype=bool)[None, :, :]
    diag_scores = jnp.where(self_mask, jnp.float32(NEG), logit_scale * diag_summed)
    pair_scores = logit_scale * pair_summed
    diag_lse = merged_lse(diag_scores, 2)
    pair_row = merged_lse(pair_scores, 2)
    col_part = merged_lse(pair_scores, 1)
    row_onehot = row_local[:, None] == jnp.arange(BPD)[None, :]
    stats_out = jnp.dot(owner_pick.T, col_part, precision=lax.Precision.HIGHEST)
    stats_out = jnp.where(jnp.sum(owner_pick, axis=0)[:, None] > 0.0, stats_out, jnp.float32(NEG))
    stats_in = lax.all_to_all(stats_out, "tensor", split_axis=0, concat_axis=0, tiled=True)
    local_cand = jnp.where(row_onehot[:, :, None], pair_row[:, None, :], jnp.float32(NEG))
    remote_cand = jnp.where(asked_sel[:, :, None] > 0.0, stats_in[:, None, :], jnp.float32(NEG))
    lse_own = merged_lse(jnp.concatenate([diag_lse[None], local_cand, remote_cand], axis=0), 0)
    lse_out = jnp.dot(asked_sel, lse_own, precision=lax.Precision.HIGHEST)
    lse_back = lax.all_to_all(lse_out, "tensor", split_axis=0, concat_axis=0, tiled=True)
    col_level = jnp.take(lse_back, col_owner, axis=0)
    row_level = jnp.take(lse_own, row_local, axis=0)
    diag_weights = (
        jnp.exp(diag_scores - lse_own[:, :, None]) + jnp.exp(diag_scores - lse_own[:, None, :])
    ).astype(jnp.bfloat16)
    pair_weights = (
        jnp.exp(pair_scores - row_level[:, :, None]) + jnp.exp(pair_scores - col_level[:, None, :])
    ).astype(jnp.bfloat16)
    diag_terms = jnp.einsum(
        "kij,kjw->kiw", diag_weights, own_blocks, preferred_element_type=jnp.float32
    )
    pair_terms = jnp.einsum(
        "kij,kjw->kiw", pair_weights, second_rows, preferred_element_type=jnp.float32
    )
    local_grad = diag_terms + jax.ops.segment_sum(pair_terms, row_local, num_segments=BPD)
    col_terms = jnp.einsum(
        "kij,kiw->kjw", pair_weights, first_rows, preferred_element_type=jnp.float32
    )
    grad_out = jax.ops.segment_sum(col_terms, col_owner, num_segments=groups)
    grad_in = lax.all_to_all(
        grad_out.astype(jnp.bfloat16), "tensor", split_axis=0, concat_axis=0, tiled=True
    ).astype(grad_out.dtype)
    remote_grad = jax.ops.segment_sum(grad_in, asked_block, num_segments=BPD)
    total_grad = (local_grad + remote_grad).reshape(rows_here, width_dev)
    partner_local = partner - group_idx * rows_here
    partner_rows = jnp.take(embeddings, partner_local, axis=0).astype(jnp.float32)
    embedding_grad = (total_grad - 2.0 * partner_rows).astype(jnp.bfloat16)
    return (lse_own.reshape(rows_here), embedding_grad)


def solution(mesh):
    in_specs = (P("tensor", "dp"), P(), P("tensor"))
    out_specs = (P("tensor"), P("tensor", "dp"))
    return jax.shard_map(
        per_device, mesh=mesh, in_specs=in_specs, out_specs=out_specs, check_vma=False
    )
```

profile of v0, /device:TPU:118, one launch (start us, length us, event | category | flops | bytes accessed | tf_op | source)
XLA Modules:
  0.0 794.0 jit_solution(10638764400180643507)
XLA Ops:
  7.2 1.4 copy.61
  8.6 0.8 reshape.213
  9.5 0.1 copy.47
  9.6 0.1 copy.48
  9.7 0.1 convert_reduce_fusion
  9.7 2.1 convolution_convert_fusion
  11.8 7.7 copy.49
  19.6 15.4 %all-to-all-start = ((bf16[64,128,448]{1,2,0:T(8,128)(2,1)}), bf16[64,128,448]{1,2,0:T(8,128)(2,1)}, u32[]{:S(2)}, u32[]{:S(2)}) async-start(bf16[64,128,448]{1,2,0:T(8,128)(2,1)} %copy.49), calls=%async_computation | async-start | bytes 14680064 | tf_op jit(solution)/shard_map/all_to_all | solution.py:54
  35.0 0.2 all-reduce.3.cloned.1.call-start
  35.2 0.8 constant_dynamic-slice_fusion
  36.0 0.0 copy-done.3
  36.0 0.2 copy_bitcast_fusion
  36.2 3.8 gather_fusion
  40.0 1.3 fusion.42
  41.3 223.6 %all-to-all-done = bf16[64,128,448]{1,2,0:T(8,128)(2,1)} async-done(((bf16[64,128,448]{1,2,0:T(8,128)(2,1)}), bf16[64,128,448]{1,2,0:T(8,128)(2,1)}, u32[]{:S(2)}, u32[]{:S(2)}) %all-to-all-start) | async-done | bytes 7340064 | tf_op jit(solution)/shard_map/all_to_all | solution.py:54
  265.0 6.9 gather_fusion.1
  271.9 8.1 %fusion.1 = f32[48,128,128]{2,1,0:T(8,128)} fusion(bf16[48,128,448]{1,2,0:T(8,128)(2,1)} %gather_fusion, pred[48]{0:T(512)(128)(4,1)S(1)} %get-tuple-element.30, bf16[48,128,448]{1,2,0:T(8,128)(2,1)} %gather_fusion.1, pred[48]{0:T(512)(128)(4,1)S(1)} %get-tuple-element.18), kind=kOutput, calls=%fused_computation.17 | convolution fusion | flops 710148096 | bytes 14155872 | tf_op jit(solution)/shard_map/kiw,kjw->kij/dot_general | solution.py:57
  279.9 0.0 all-reduce.3.cloned.1.call-update
  280.0 0.1 copy.50
  280.1 0.1 convert_reduce_fusion.1
  280.2 0.1 iota_compare_fusion.4
  280.3 98.5 %all-reduce.3.cloned.1.call-done = (f32[48,128,128]{2,1,0:T(8,128)}, f32[8,128,128]{2,1,0:T(8,128)}) async-done(((f32[48,128,128]{2,1,0:T(8,128)}, f32[8,128,128]{2,1,0:T(8,128)}), (f32[48,128,128]{2,1,0:T(8,128)}, f32[8,128,128]{2,1,0:T(8,128)})) %all-reduce.3.cloned.1.call-update) | async-done | bytes 3670032 | tf_op jit(solution)/shard_map/psum | solution.py:60
  378.8 2.9 multiply_reduce_fusion.1
  381.7 0.0 copy-done.1
  381.7 2.0 exponential_reduce_fusion.1
  383.7 0.7 exponential_reduce_fusion
  384.4 0.9 convolution_select_fusion
  385.3 13.1 %all-to-all-start.1 = ((f32[64,1,128]{2,1,0:T(1,128)}), f32[64,1,128]{2,1,0:T(1,128)S(1)}, u32[]{:S(2)}, u32[]{:S(2)}) async-start(f32[64,1,128]{2,1,0:T(1,128)} %bitcast.10), calls=%async_computation.1 | async-start | bytes 65536 | tf_op jit(solution)/shard_map/all_to_all | solution.py:70
  398.4 1.3 fusion.6
  399.7 0.1 broadcast_select_fusion.7
  399.8 1.4 exponential_reduce_fusion.2
  401.2 5.2 all-to-all-done.1
  406.4 0.1 broadcast_select_fusion.6
  406.6 0.1 fusion.5
  406.7 0.0 copy-start.5
  406.7 0.9 fusion.45
  407.6 0.6 gather_fusion.2
  408.1 8.5 %all-to-all-start.2 = ((f32[64,1,128]{2,1,0:T(1,128)}), f32[64,1,128]{2,1,0:T(1,128)S(1)}, u32[]{:S(2)}, u32[]{:S(2)}) async-start(f32[64,1,128]{2,1,0:T(1,128)} %bitcast.15), calls=%async_computation.2 | async-start | bytes 65536 | tf_op jit(solution)/shard_map/all_to_all | solution.py:75
  416.7 0.1 broadcast_select_fusion.9
  416.7 8.0 %all-to-all-done.2 = f32[64,1,128]{2,1,0:T(1,128)S(1)} async-done(((f32[64,1,128]{2,1,0:T(1,128)}), f32[64,1,128]{2,1,0:T(1,128)S(1)}, u32[]{:S(2)}, u32[]{:S(2)}) %all-to-all-start.2) | async-done | bytes 32800 | tf_op jit(solution)/shard_map/all_to_all | solution.py:75
  424.7 0.6 gather_fusion.3
  425.3 0.1 broadcast_select_fusion.8
  425.3 7.0 fusion
  432.3 7.0 broadcast_in_dim.166
  439.3 26.5 %scatter_fusion.1 = f32[64,128,448]{1,2,0:T(8,128)} fusion(f32[64,128,448]{1,2,0:T(8,128)} %broadcast_in_dim.166, s32[48]{0:T(128)S(1)} %bitcast.85, f32[48,128,448]{1,2,0:T(8,128)} %fusion), kind=kCustom, calls=%fused_computation.6 | custom fusion | flops 2752512 | bytes 33030336 | tf_op jit(solution)/shard_map/scatter-add | solution.py:94
  465.8 9.4 %convert_element_type.36 = bf16[64,128,448]{1,2,0:T(8,128)(2,1)} convert(f32[64,128,448]{1,2,0:T(8,128)} %scatter_fusion.1) | non-fusion elementwise | flops 3670016 | bytes 22020096 | tf_op jit(solution)/shard_map/convert_element_type | solution.py:96
  475.2 9.9 %all-to-all-start.3 = ((bf16[64,128,448]{1,2,0:T(8,128)(2,1)}), bf16[64,128,448]{1,2,0:T(8,128)(2,1)}, u32[]{:S(2)}, u32[]{:S(2)}) async-start(bf16[64,128,448]{1,2,0:T(8,128)(2,1)} %convert_element_type.36), calls=%async_computation.3 | async-start | bytes 14680064 | tf_op jit(solution)/shard_map/all_to_all | solution.py:95
  485.2 0.0 copy-done.4
  485.2 0.5 copy.55
  485.7 0.1 fusion.20
  485.9 0.1 reduce_or.9
  486.0 5.1 gather_fusion.4
  491.1 1.7 fusion.7
  492.8 0.3 copy-done.2
  493.1 7.0 fusion.2
  500.1 16.1 %scatter_fusion = f32[8,128,448]{1,2,0:T(8,128)S(1)} fusion(f32[8,128,448]{1,2,0:T(8,128)S(1)} %fusion.7, s32[48]{0:T(128)S(1)} %get-tuple-element.28, f32[48,128,448]{1,2,0:T(8,128)} %fusion.2), kind=kCustom, calls=%fused_computation.5 | custom fusion | flops 2752512 | bytes 33030336 | tf_op jit(solution)/shard_map/scatter-add | solution.py:90
  516.2 230.9 %all-to-all-done.3 = bf16[64,128,448]{1,2,0:T(8,128)(2,1)} async-done(((bf16[64,128,448]{1,2,0:T(8,128)(2,1)}), bf16[64,128,448]{1,2,0:T(8,128)(2,1)}, u32[]{:S(2)}, u32[]{:S(2)}) %all-to-all-start.3) | async-done | bytes 7340064 | tf_op jit(solution)/shard_map/all_to_all | solution.py:95
  747.1 10.2 %convert_element_type.37 = f32[64,128,448]{1,2,0:T(8,128)} convert(bf16[64,128,448]{1,2,0:T(8,128)(2,1)} %all-to-all-done.3) | non-fusion elementwise | flops 3670016 | bytes 22020096 | tf_op jit(solution)/shard_map/convert_element_type | solution.py:97
  757.3 0.1 broadcast.142
  757.4 21.2 %scatter_fusion.2 = f32[8,128,448]{1,2,0:T(8,128)S(1)} fusion(f32[8,128,448]{1,2,0:T(8,128)S(1)} %broadcast.142, s32[64]{0:T(128)S(1)} %broadcast_select_fusion.10, f32[64,128,448]{1,2,0:T(8,128)} %convert_element_type.37), kind=kCustom, calls=%fused_computation.7 | custom fusion | flops 3670016 | bytes 44040448 | tf_op jit(solution)/shard_map/scatter-add | solution.py:98
  778.6 2.9 add.148
  781.6 2.0 copy.58
  783.6 1.4 fusion.3
  784.9 2.2 copy.57
  (27 shorter events, 0.2 us)
Async XLA Ops:
  19.6 16.4 %copy-start.3 = (bf16[1024,448]{0,1:T(8,128)(2,1)S(1)}, bf16[1024,448]{0,1:T(8,128)(2,1)}, u32[]{:S(2)}) copy-start(bf16[1024,448]{0,1:T(8,128)(2,1)} %param.3) | copy-start | bytes 2752516
  19.6 245.4 %all-to-all-start = ((bf16[64,128,448]{1,2,0:T(8,128)(2,1)}), bf16[64,128,448]{1,2,0:T(8,128)(2,1)}, u32[]{:S(2)}, u32[]{:S(2)}) async-start(bf16[64,128,448]{1,2,0:T(8,128)(2,1)} %copy.49), calls=%async_computation | async-start | bytes 14680064 | tf_op jit(solution)/shard_map/all_to_all | solution.py:54
  35.0 343.8 %all-reduce.3.cloned.1.call-start = ((), (), s32[]{:S(2)}) async-start(), calls=%async_computation.4 | async-start | bytes 7340032 | tf_op jit(solution)/shard_map/psum | solution.py:60
  378.8 2.9 copy-start.1
  385.3 21.1 %all-to-all-start.1 = ((f32[64,1,128]{2,1,0:T(1,128)}), f32[64,1,128]{2,1,0:T(1,128)S(1)}, u32[]{:S(2)}, u32[]{:S(2)}) async-start(f32[64,1,128]{2,1,0:T(1,128)} %bitcast.10), calls=%async_computation.1 | async-start | bytes 65536 | tf_op jit(solution)/shard_map/all_to_all | solution.py:70
  406.7 84.4 %copy-start.5 = (f32[8,128]{1,0:T(8,128)}, f32[8,128]{1,0:T(8,128)S(1)}, u32[]{:S(2)}) copy-start(f32[8,128]{1,0:T(8,128)S(1)} %log_add_fusion.1) | copy-start | bytes 12292
  408.1 16.5 %all-to-all-start.2 = ((f32[64,1,128]{2,1,0:T(1,128)}), f32[64,1,128]{2,1,0:T(1,128)S(1)}, u32[]{:S(2)}, u32[]{:S(2)}) async-start(f32[64,1,128]{2,1,0:T(1,128)} %bitcast.15), calls=%async_computation.2 | async-start | bytes 65536 | tf_op jit(solution)/shard_map/all_to_all | solution.py:75
  475.2 9.9 %copy-start.4 = (bf16[1024,448]{0,1:T(8,128)(2,1)S(1)}, bf16[1024,448]{0,1:T(8,128)(2,1)}, u32[]{:S(2)}) copy-start(bf16[1024,448]{0,1:T(8,128)(2,1)} %param.3) | copy-start | bytes 2752516
  475.2 10.7 %copy-start.7 = (s32[1024]{0:T(1024)S(1)}, s32[1024]{0:T(1024)}, u32[]{:S(2)}) copy-start(s32[1024]{0:T(1024)} %param.5) | copy-start | bytes 12292
  475.2 271.8 %all-to-all-start.3 = ((bf16[64,128,448]{1,2,0:T(8,128)(2,1)}), bf16[64,128,448]{1,2,0:T(8,128)(2,1)}, u32[]{:S(2)}, u32[]{:S(2)}) async-start(bf16[64,128,448]{1,2,0:T(8,128)(2,1)} %convert_element_type.36), calls=%async_computation.3 | async-start | bytes 14680064 | tf_op jit(solution)/shard_map/all_to_all | solution.py:95
  491.1 2.0 copy-start.2
  516.2 230.9 %copy-start = (f32[8,128,448]{1,2,0:T(8,128)}, f32[8,128,448]{1,2,0:T(8,128)S(1)}, u32[]{:S(2)}) copy-start(f32[8,128,448]{1,2,0:T(8,128)S(1)} %scatter_fusion) | copy-start | bytes 5505028
  781.6 2.0 copy-start.6
Sparse Core Ops, SparseCore 0:
  280.1 98.6 all-reduce.2
where the time goes:
time: 795 us; the launch traced here: 794 us
  waiting for transfers between devices  566 us (71%)
  other arithmetic  97.2 us (12%)
  starting transfers between devices  47.1 us (6%)
  local copies, waits for them, and re-layouts  40.3 us (5%)
  matrix products  28.8 us (4%)
  between operations  14.3 us (2%)
    all_to_all x1, waiting for transfers between devices, per_device(): lax.all_to_all(grad_out.astype(jnp.bfloat16), 'tensor', split_axis=0, con...  231 us
    all_to_all x1, waiting for transfers between devices, per_device(): lax.all_to_all(outgoing, 'tensor', split_axis=0, concat_axis=0, tiled=True)  224 us
    psum x1, waiting for transfers between devices, per_device(): diag_summed, pair_summed = lax.psum((diag_partial, pair_partial), 'dp')  98.5 us
    scatter-add x1, other arithmetic, per_device(): grad_out = jax.ops.segment_sum(col_terms, col_owner, num_segments=groups)  26.5 us
    scatter-add x1, other arithmetic, per_device(): remote_grad = jax.ops.segment_sum(grad_in, asked_block, num_segments=BPD)  21.2 us
    scatter-add x1, other arithmetic, per_device(): jax.ops.segment_sum(pair_terms, row_local, num_segments=BPD)  16.1 us
  transfers between devices with their start and end apart: 5, of which 5 were waited for; matrix products, arithmetic and copies ran while one was open for 5% of the time, Pallas kernels for 0%

commit v1 on v0

v1 whole, which is shorter than its diff:
```python
import math

import jax
import jax.numpy as jnp
from jax import lax
from jax.sharding import PartitionSpec as P

D = 3584
BPD = 8
NEG = -1e30


def merged_lse(values, axis):
    top = jnp.max(values, axis=axis, keepdims=True)
    total = jnp.sum(jnp.exp(values - top), axis=axis, keepdims=True)
    return jnp.squeeze(top + jnp.log(total), axis=axis)


def slot_tables(pairs, group_idx, side):
    groups = side * side
    per_group = pairs.shape[0] // groups
    z_here, y_here = group_idx // side, group_idx % side
    rows = lax.dynamic_slice_in_dim(
        pairs.reshape(side, side, per_group, 2), z_here, 1, 0
    )[0]
    owner = rows[:, :, 1] // BPD
    wanted = jnp.arange(side) * side + y_here
    match = owner[:, None, :] == wanted[None, :, None]
    first = jnp.sum(jnp.where(match, rows[:, None, :, 0] % BPD, 0), axis=2)
    second = jnp.sum(jnp.where(match, rows[:, None, :, 1] % BPD, 0), axis=2)
    return first, second, jnp.any(match, axis=2)


def per_device(embeddings, pairs, partner):
    rows_here, width_dev = embeddings.shape
    groups = lax.axis_size("tensor")
    side = math.isqrt(groups)
    group_idx = lax.axis_index("tensor")
    block_len = rows_here // BPD
    logit_scale = 2.0 / math.sqrt(D)
    along_y = [[z * side + y for y in range(side)] for z in range(side)]
    along_z = [[z * side + y for z in range(side)] for y in range(side)]
    own_blocks = embeddings.reshape(BPD, block_len, width_dev)
    first, second, valid = slot_tables(pairs, group_idx, side)

    row_blocks = lax.all_gather(own_blocks, "tensor", axis_index_groups=along_y)
    col_blocks = lax.all_gather(own_blocks, "tensor", axis_index_groups=along_z)
    diag_partial = jnp.einsum(
        "kiw,kjw->kij", own_blocks, own_blocks, preferred_element_type=jnp.float32
    )
    lane = jnp.arange(side)
    first_rows = row_blocks[lane[:, None], first]
    second_rows = col_blocks[lane[None, :], second]
    pair_partial = jnp.einsum(
        "yziw,yzjw->yzij", first_rows, second_rows, preferred_element_type=jnp.float32
    )
    diag_summed, pair_summed = lax.psum((diag_partial, pair_partial), "dp")
    self_mask = jnp.eye(block_len, dtype=bool)[None, :, :]
    diag_scores = jnp.where(self_mask, jnp.float32(NEG), logit_scale * diag_summed)
    pair_scores = logit_scale * pair_summed
    diag_lse = merged_lse(diag_scores, 2)
    row_part = merged_lse(pair_scores, 3)
    col_part = merged_lse(pair_scores, 2)
    ids = jnp.arange(BPD)
    row_hot = (first[:, :, None] == ids) & valid[:, :, None]
    col_hot = (second[:, :, None] == ids) & valid[:, :, None]
    row_stats = merged_lse(
        jnp.where(row_hot[..., None], row_part[:, :, None, :], jnp.float32(NEG)), 1
    )
    col_stats = merged_lse(
        jnp.where(col_hot[..., None], col_part[:, :, None, :], jnp.float32(NEG)), 0
    )
    row_in = lax.all_to_all(
        row_stats, "tensor", 0, 0, axis_index_groups=along_y, tiled=True
    )
    col_in = lax.all_to_all(
        col_stats, "tensor", 0, 0, axis_index_groups=along_z, tiled=True
    )
    lse_own = merged_lse(jnp.concatenate([diag_lse[None], row_in, col_in], axis=0), 0)
    row_lse = lax.all_gather(lse_own, "tensor", axis_index_groups=along_y)
    col_lse = lax.all_gather(lse_own, "tensor", axis_index_groups=along_z)
    row_level = row_lse[lane[:, None], first]
    col_level = col_lse[lane[None, :], second]
    diag_weights = (
        jnp.exp(diag_scores - lse_own[:, :, None]) + jnp.exp(diag_scores - lse_own[:, None, :])
    ).astype(jnp.bfloat16)
    pair_weights = jnp.where(
        valid[:, :, None, None],
        jnp.exp(pair_scores - row_level[..., :, None])
        + jnp.exp(pair_scores - col_level[..., None, :]),
        0.0,
    ).astype(jnp.bfloat16)
    diag_terms = jnp.einsum(
        "kij,kjw->kiw", diag_weights, own_blocks, preferred_element_type=jnp.float32
    )
    zero = jnp.bfloat16(0)
    wide_row = jnp.where(row_hot[..., None, None], pair_weights[:, :, None], zero)
    wide_col = jnp.where(col_hot[..., None, None], pair_weights[:, :, None], zero)
    row_terms = jnp.einsum(
        "yzkij,yzjw->ykiw", wide_row, second_rows, preferred_element_type=jnp.float32
    ).astype(jnp.bfloat16)
    col_terms = jnp.einsum(
        "yzkij,yziw->zkjw", wide_col, first_rows, preferred_element_type=jnp.float32
    ).astype(jnp.bfloat16)
    row_grad = lax.psum_scatter(row_terms, "tensor", axis_index_groups=along_y)
    col_grad = lax.psum_scatter(col_terms, "tensor", axis_index_groups=along_z)
    total = diag_terms + row_grad.astype(jnp.float32) + col_grad.astype(jnp.float32)
    total = total.reshape(rows_here, width_dev)
    partner_local = partner - group_idx * rows_here
    partner_rows = jnp.take(embeddings, partner_local, axis=0).astype(jnp.float32)
    embedding_grad = (total - 2.0 * partner_rows).astype(jnp.bfloat16)
    return (lse_own.reshape(rows_here), embedding_grad)


def solution(mesh):
    in_specs = (P("tensor", "dp"), P(), P("tensor"))
    out_specs = (P("tensor"), P("tensor", "dp"))
    return jax.shard_map(
        per_device, mesh=mesh, in_specs=in_specs, out_specs=out_specs, check_vma=False
    )
```

time: 795 us -> 581 us (0.73)
  the two profiles are of different devices: /device:TPU:118 before, /device:TPU:1 now
where the time goes in v1:
time: 581 us; the launch traced here: 580 us
  waiting for transfers between devices  427 us (73%)
  matrix products  41 us (7%)
  blocking collectives  36.4 us (6%)
  local copies, waits for them, and re-layouts  33.1 us (6%)
  other arithmetic  15.1 us (3%)
  between operations  14.1 us (2%)
  starting transfers between devices  13.8 us (2%)
    all_gather x1, waiting for transfers between devices, per_device(): row_blocks = lax.all_gather(own_blocks, 'tensor', axis_index_groups=along_y)  90.1 us
    reduce_scatter x1, waiting for transfers between devices, per_device(): row_grad = lax.psum_scatter(row_terms, 'tensor', axis_index_groups=along_y)  88.1 us
    all_gather x1, waiting for transfers between devices, per_device(): col_blocks = lax.all_gather(own_blocks, 'tensor', axis_index_groups=along_z)  81.9 us
    psum x1, waiting for transfers between devices, per_device(): diag_summed, pair_summed = lax.psum((diag_partial, pair_partial), 'dp')  81.4 us
    reduce_scatter x1, waiting for transfers between devices, per_device(): col_grad = lax.psum_scatter(col_terms, 'tensor', axis_index_groups=along_z)  72.2 us
    all_gather x1, blocking collectives, per_device(): row_lse = lax.all_gather(lse_own, 'tensor', axis_index_groups=along_y)  18.3 us
    all_gather x1, blocking collectives, per_device(): col_lse = lax.all_gather(lse_own, 'tensor', axis_index_groups=along_z)  18.1 us
    dot_general x1, matrix products, per_device(): jnp.einsum('yzkij,yziw->zkjw', wide_col, first_rows, preferred_element_ty...  14.4 us
  transfers between devices with their start and end apart: 7, of which 7 were waited for; matrix products, arithmetic and copies ran while one was open for 6% of the time, Pallas kernels for 0%

profile of v1, /device:TPU:1, one launch (start us, length us, event | category | flops | bytes accessed | tf_op | source)
XLA Modules:
  0.0 580.1 jit_solution(14007736566668007151)
XLA Ops:
  7.2 0.0 copy-start.1
  7.2 0.0 copy-start.6
  7.2 0.0 all-gather.3.cloned.1.call-start
  7.2 1.5 copy.95
  8.7 1.1 copy.72
  9.8 0.0 all-gather.3.cloned.1.call-update
  9.8 0.0 all-gather.5.cloned.1.call-start
  9.9 0.7 all-gather.5.cloned.1.call-update
  10.6 0.0 all-reduce.3.cloned.1.call-start
  10.6 0.1 reshape.310
  10.8 0.4 fusion.38
  11.2 0.1 reshape.315
  11.3 0.1 reshape.321
  11.4 1.3 fusion.21
  12.7 90.1 %all-gather.3.cloned.1.call-done = bf16[8,8,128,448]{2,3,1,0:T(8,128)(2,1)} async-done(((bf16[1,8,128,448]{2,3,1,0:T(8,128)(2,1)}), bf16[8,8,128,448]{2,3,1,0:T(8,128)(2,1)}) %all-gather.3.cloned.1.call-update) | async-done | bytes 7340048 | tf_op jit(solution)/shard_map/all_gather | solution.py:46
  102.8 7.5 %gather_fusion = bf16[64,128,448]{1,2,0:T(8,128)(2,1)} fusion(bf16[8,8,128,448]{2,3,1,0:T(8,128)(2,1)} %all-gather.3.cloned.1.call-done, s32[64]{0:T(128)S(1)} %reshape.315), kind=kCustom, calls=%fused_computation | custom fusion | bytes 14680576 | tf_op jit(solution)/shard_map/gather | solution.py:52
  110.4 81.9 %all-gather.5.cloned.1.call-done = bf16[8,8,128,448]{2,3,1,0:T(8,128)(2,1)} async-done(((bf16[1,8,128,448]{2,3,1,0:T(8,128)(2,1)}), bf16[8,8,128,448]{2,3,1,0:T(8,128)(2,1)}) %all-gather.5.cloned.1.call-update) | async-done | bytes 7340048 | tf_op jit(solution)/shard_map/all_gather | solution.py:47
  192.3 7.6 %gather_fusion.1 = bf16[64,128,448]{1,2,0:T(8,128)(2,1)} fusion(bf16[8,8,128,448]{2,3,1,0:T(8,128)(2,1)} %all-gather.5.cloned.1.call-done, s32[64]{0:T(128)S(1)} %reshape.321), kind=kCustom, calls=%fused_computation.1 | custom fusion | bytes 14680576 | tf_op jit(solution)/shard_map/gather | solution.py:53
  199.9 9.6 %fusion.58 = f32[8,8,128,128]{3,2,1,0:T(8,128)} fusion(bf16[8,8,128,448]{2,3,1,0:T(8,128)(2,1)} %bitcast.96, bf16[8,8,128,448]{2,3,1,0:T(8,128)(2,1)} %bitcast.94), kind=kOutput, calls=%fused_computation.107 | convolution fusion | flops 939524096 | bytes 18874368 | tf_op jit(solution)/shard_map/yziw,yzjw->yzij/dot_general | solution.py:54
  209.5 0.0 all-reduce.3.cloned.1.call-update
  209.5 0.3 compare_reduce_fusion
  209.8 0.1 fusion.39
  209.9 0.1 copy.79
  210.1 81.4 %all-reduce.3.cloned.1.call-done = (f32[8,8,128,128]{3,2,1,0:T(8,128)}, f32[8,128,128]{2,1,0:T(8,128)}) async-done(((f32[8,8,128,128]{3,2,1,0:T(8,128)}, f32[8,128,128]{2,1,0:T(8,128)}), (f32[8,8,128,128]{3,2,1,0:T(8,128)}, f32[8,128,128]{2,1,0:T(8,128)})) %all-reduce.3.cloned.1.call-update) | async-done | bytes 4718608 | tf_op jit(solution)/shard_map/psum | solution.py:57
  291.5 3.5 multiply_reduce_fusion.1
  295.0 2.6 exponential_reduce_fusion.1
  297.6 1.0 exponential_reduce_fusion
  298.7 0.1 select_reduce_fusion
  298.8 0.1 fusion.29
  299.0 0.6 log_add_fusion
  299.6 7.1 %all-to-all-start.1 = ((f32[8,8,128]{2,1,0:T(8,128)}), f32[8,8,128]{2,1,0:T(8,128)S(1)}, u32[]{:S(2)}, u32[]{:S(2)}) async-start(f32[8,8,128]{2,1,0:T(8,128)} %log_add_fusion), calls=%async_computation.1 | async-start | bytes 65536 | tf_op jit(solution)/shard_map/all_to_all | solution.py:76
  306.7 0.1 select_reduce_fusion.1
  306.8 0.1 fusion.27
  307.0 0.6 log_add_fusion.2
  307.6 0.2 fusion.25
  307.8 5.8 all-to-all-done.1
  313.6 6.5 %all-to-all-start = ((f32[8,8,128]{2,1,0:T(8,128)}), f32[8,8,128]{2,1,0:T(8,128)S(1)}, u32[]{:S(2)}, u32[]{:S(2)}) async-start(f32[8,8,128]{2,1,0:T(8,128)} %log_add_fusion.2), calls=%async_computation | async-start | bytes 65536 | tf_op jit(solution)/shard_map/all_to_all | solution.py:73
  320.0 0.0 reduce-scatter.5.cloned.1.call-start
  320.1 0.4 exponential_reduce_fusion.2
  320.5 6.4 %all-to-all-done = f32[8,8,128]{2,1,0:T(8,128)S(1)} async-done(((f32[8,8,128]{2,1,0:T(8,128)}), f32[8,8,128]{2,1,0:T(8,128)S(1)}, u32[]{:S(2)}, u32[]{:S(2)}) %all-to-all-start) | async-done | bytes 32800 | tf_op jit(solution)/shard_map/all_to_all | solution.py:73
  326.9 0.6 copy-done.5
  327.6 18.1 %all_gather.15 = f32[8,8,128]{2,1,0:T(8,128)S(1)} all-gather(f32[1,8,128]{2,1,0:T(8,128)S(1)} %bitcast_add_fusion), channel_id=1, replica_groups={{0,8,16,24,32,40,48,56},{1,9,17,25,33,41,49,57},{2,10,18,26,34,42,50,58..., dimensions={0}, use_global_device_ids=true | all-gather | bytes 36864 | tf_op jit(solution)/shard_map/all_gather | solution.py:81
  345.7 18.3 %all_gather.14 = f32[8,8,128]{2,1,0:T(8,128)S(1)} all-gather(f32[1,8,128]{2,1,0:T(8,128)S(1)} %bitcast_add_fusion), channel_id=1, replica_groups={{0,1,2,3,4,5,6,7},{8,9,10,11,12,13,14,15},{16,17,18,19,20,21,22,23},{24..., dimensions={0}, use_global_device_ids=true | all-gather | bytes 36864 | tf_op jit(solution)/shard_map/all_gather | solution.py:80
  363.9 0.8 gather_fusion.3
  364.7 0.8 gather_fusion.2
  365.5 14.4 %bitcast_convert_fusion = bf16[8,8,128,448]{2,3,1,0:T(8,128)(2,1)} fusion(pred[8,8,8]{0,2,1:T(8,128)(4,1)S(1)} %copy.79, bf16[8,8,128,448,1]{2,3,1,0,4:T(8,128)(2,1)} %bitcast.97, f32[8,8,128,128]{3,2,1,0:T(8,128)} %get-tuple-element.16, f32[8,8,128]{2,1,0:T(8,128)S(1)} %bitcast.101, f32[8,8,128]{2,1,0:T(8,128)S(1)} %bitcast.103, ...), kind=kOutput, calls=%fused_computation.11 | convolution fusion | flops 7534542848 | bytes 18940480 | tf_op jit(solution)/shard_map/yzkij,yziw->zkjw/dot_general | solution.py:102
  379.8 0.0 reduce-scatter.5.cloned.1.call-update
  379.8 0.0 reduce-scatter.3.cloned.1.call-start
  379.9 0.1 copy.75
  380.0 12.5 %fusion.10 = bf16[8,8,128,448]{2,3,0,1:T(8,128)(2,1)S(1)} fusion(pred[8,8,8]{0,2,1:T(8,128)(4,1)S(1)} %copy.75, bf16[8,8,128,448,1]{2,3,1,0,4:T(8,128)(2,1)} %bitcast.95, f32[8,8,128,128]{3,2,1,0:T(8,128)} %get-tuple-element.16, f32[8,8,128]{2,1,0:T(8,128)S(1)} %bitcast.102, f32[8,8,128]{2,1,0:T(8,128)S(1)} %bitcast.104, ...), kind=kOutput, calls=%fused_computation.17 | convolution fusion | flops 7530872832 | bytes 18940480 | tf_op jit(solution)/shard_map/yzkij,yzjw->ykiw/dot_general | solution.py:99
  392.5 3.6 copy.111
  396.1 0.0 reduce-scatter.3.cloned.1.call-update
  396.1 0.5 copy.82
  396.6 0.1 copy-done.7
  396.8 0.6 fusion.50
  397.4 4.4 gather_fusion.4
  401.8 1.3 compare_and_fusion
  403.1 0.7 log_add_fusion.5
  403.8 72.2 %reduce-scatter.5.cloned.1.call-done = bf16[1,8,128,448]{2,3,1,0:T(8,128)(2,1)} async-done(((bf16[8,8,128,448]{2,3,1,0:T(8,128)(2,1)}), bf16[1,8,128,448]{2,3,1,0:T(8,128)(2,1)}) %reduce-scatter.5.cloned.1.call-update) | async-done | bytes 917520 | tf_op jit(solution)/shard_map/reduce_scatter | solution.py:106
  476.1 88.1 %reduce-scatter.3.cloned.1.call-done = bf16[1,8,128,448]{2,3,1,0:T(8,128)(2,1)} async-done(((bf16[8,8,128,448]{2,3,1,0:T(8,128)(2,1)}), bf16[1,8,128,448]{2,3,1,0:T(8,128)(2,1)}) %reduce-scatter.3.cloned.1.call-update) | async-done | bytes 917520 | tf_op jit(solution)/shard_map/reduce_scatter | solution.py:105
  564.2 3.2 convert_add_fusion
  567.5 1.9 copy.92
  569.3 2.1 fusion.19
  571.4 2.2 copy.84
  (25 shorter events, 0.2 us)
Async XLA Ops:
  7.2 4.3 copy-start.1
  7.2 3.5 copy-start.6
  7.2 95.7 %all-gather.3.cloned.1.call-start = ((), (), s32[]{:S(2)}) async-start(), calls=%async_computation.4 | async-start | bytes 8257536 | tf_op jit(solution)/shard_map/all_gather | solution.py:46
  9.8 182.5 %all-gather.5.cloned.1.call-start = ((), (), s32[]{:S(2)}) async-start(), calls=%async_computation.5 | async-start | bytes 8257536 | tf_op jit(solution)/shard_map/all_gather | solution.py:47
  10.6 280.9 %all-reduce.3.cloned.1.call-start = ((), (), s32[]{:S(2)}) async-start(), calls=%async_computation.8 | async-start | bytes 9437184 | tf_op jit(solution)/shard_map/psum | solution.py:57
  291.5 3.5 copy-start
  295.0 12.6 %copy-start.2 = (f32[8,128,128]{2,1,0:T(8,128)S(1)}, f32[8,128,128]{2,1,0:T(8,128)}, u32[]{:S(2)}) copy-start(f32[8,128,128]{2,1,0:T(8,128)} %get-tuple-element.17) | copy-start | bytes 1572868
  299.6 14.0 %all-to-all-start.1 = ((f32[8,8,128]{2,1,0:T(8,128)}), f32[8,8,128]{2,1,0:T(8,128)S(1)}, u32[]{:S(2)}, u32[]{:S(2)}) async-start(f32[8,8,128]{2,1,0:T(8,128)} %log_add_fusion), calls=%async_computation.1 | async-start | bytes 65536 | tf_op jit(solution)/shard_map/all_to_all | solution.py:76
  313.6 13.3 %all-to-all-start = ((f32[8,8,128]{2,1,0:T(8,128)}), f32[8,8,128]{2,1,0:T(8,128)S(1)}, u32[]{:S(2)}, u32[]{:S(2)}) async-start(f32[8,8,128]{2,1,0:T(8,128)} %log_add_fusion.2), calls=%async_computation | async-start | bytes 65536 | tf_op jit(solution)/shard_map/all_to_all | solution.py:73
  320.0 156.0 %reduce-scatter.5.cloned.1.call-start = ((), (), s32[]{:S(2)}) async-start(), calls=%async_computation.7 | async-start | bytes 8257536 | tf_op jit(solution)/shard_map/reduce_scatter | solution.py:106
  326.9 0.6 copy-start.5
  327.5 52.3 %copy-start.4 = (f32[8,128]{1,0:T(8,128)}, f32[8,128]{1,0:T(8,128)S(1)}, u32[]{:S(2)}) copy-start(f32[8,128]{1,0:T(8,128)S(1)} %fusion.36) | copy-start | bytes 12292
  379.8 184.4 %reduce-scatter.3.cloned.1.call-start = ((), (), s32[]{:S(2)}) async-start(), calls=%async_computation.6 | async-start | bytes 8257536 | tf_op jit(solution)/shard_map/reduce_scatter | solution.py:105
  396.1 0.7 copy-start.7
  403.8 160.4 %copy-start.3 = (f32[8,128]{1,0:T(8,128)}, f32[8,128]{1,0:T(8,128)S(1)}, u32[]{:S(2)}) copy-start(f32[8,128]{1,0:T(8,128)S(1)} %log_add_fusion.5) | copy-start | bytes 12292
Sparse Core Ops, SparseCore 0:
  10.7 92.1 all-gather.2
  105.5 86.7 all-gather.4
  209.7 81.7 all-reduce.2
  380.0 96.0 reduce-scatter.4
  478.7 85.4 reduce-scatter.2

commit v2 on v1

v2 whole, which is shorter than its diff:
```python
import functools
import math

import jax
import jax.numpy as jnp
from jax import lax
from jax.experimental import pallas as pl
from jax.experimental.pallas import tpu as pltpu
from jax.sharding import PartitionSpec as P

D = 3584
BPD = 8
BLK = 128
HALF_BPD = BPD // 2
NEG = -1e30
VMEM_BYTES = 63 * 1024 * 1024
MESH = pl.DeviceIdType.MESH
F32 = jnp.float32
BF16 = jnp.bfloat16


def ring_distance(rel, side):
    return min(rel, side - rel)


def slot_plan(side):
    batches = []
    for step in range(1, side // 2 + 1):
        batches.append(
            [
                (ry, rz)
                for ry in range(side)
                for rz in range(side)
                if max(ring_distance(ry, side), ring_distance(rz, side)) == step
            ]
        )
    return batches


def slot_tables(pairs, group_idx, side):
    groups = side * side
    per_group = pairs.shape[0] // groups
    z_here, y_here = group_idx // side, group_idx % side
    rows = lax.dynamic_slice_in_dim(
        pairs.reshape(side, side, per_group, 2), z_here, 1, 0
    )[0]
    order = [slot for batch in slot_plan(side) for slot in batch]
    ry = jnp.array([slot[0] for slot in order], jnp.int32)
    rz = jnp.array([slot[1] for slot in order], jnp.int32)
    source = rows[(y_here + ry) % side]
    wanted = ((z_here + rz) % side) * side + y_here
    match = source[:, :, 1] // BPD == wanted[:, None]
    listed = jnp.any(match, axis=1)
    first = jnp.sum(jnp.where(match, source[:, :, 0] % BPD, 0), axis=1)
    second = jnp.sum(jnp.where(match, source[:, :, 1] % BPD, 0), axis=1)
    first = jnp.where(listed, first, -1)
    second = jnp.where(listed, second, -1)
    return jnp.stack([first, second, ry, rz]).astype(jnp.int32)


def lse_rows(values):
    top = jnp.max(values, axis=0, keepdims=True)
    return top + jnp.log(jnp.sum(jnp.exp(values - top), axis=0, keepdims=True))


def merge(parts):
    top = functools.reduce(jnp.maximum, parts)
    return top + jnp.log(functools.reduce(jnp.add, [jnp.exp(p - top) for p in parts]))


def kernel(side, xs, scale, *refs):
    half = side // 2
    plan = slot_plan(side)
    counts = [BPD] + [len(batch) for batch in plan]
    nb = len(counts)
    pos = {slot: i for i, slot in enumerate(s for batch in plan for s in batch)}
    base = [0]
    for batch in plan:
        base.append(base[-1] + len(batch))
    events = 2 * half - 1

    refs = list(refs)

    def take(n):
        out = refs[:n]
        del refs[:n]
        return out

    emb, tab, partner, lse_out, grad_out = take(5)
    rowbuf = [emb] + take(side - 1)
    colbuf = [emb] + take(side - 1)
    part = take(nb)
    from_core = take(nb)
    from_x = take(nb)
    score = take(nb)
    (row_stat, col_stat, diag_stat, stat_send, stat_recv, level, w_ref, wt_ref) = take(8)
    (wide, stacked, temp, acc, fresh) = take(5)
    ring_in = [take(events) for _ in range(4)]
    (ag_send, ag_recv, c1_send, c1_recv, x2_send, x2_recv, x3_send, x3_recv) = take(8)
    (c4_send, c4_recv, l_send, l_recv, rs_send, rs_recv) = take(6)

    me = lax.axis_index("tensor")
    d = lax.axis_index("dp")
    z_here, y_here = lax.div(me, side), lax.rem(me, side)
    x_here, core = lax.div(d, 2), lax.rem(d, 2)
    other = 1 - core

    def at_y(r):
        return {"dp": d, "tensor": z_here * side + lax.rem(y_here + r, side)}

    def at_z(r):
        return {"dp": d, "tensor": lax.rem(z_here + r, side) * side + y_here}

    def x_of(r):
        return lax.rem(x_here + r, xs)

    def at_x(r):
        return {"dp": x_of(r) * 2 + core, "tensor": me}

    at_core = {"dp": x_here * 2 + other, "tensor": me}
    peers = [at_y(r) for r in range(1, side)] + [at_z(r) for r in range(1, side)]
    peers += [at_x(r) for r in range(1, xs)] + [at_core]
    barrier = pltpu.get_barrier_semaphore()
    for peer in peers:
        pl.semaphore_signal(barrier, inc=1, device_id=peer, device_id_type=MESH)
    pl.semaphore_wait(barrier, len(peers))

    started = []

    def send(src, dst, send_sem, recv_sem, device):
        copy = pltpu.make_async_remote_copy(
            src_ref=src,
            dst_ref=dst,
            send_sem=send_sem,
            recv_sem=recv_sem,
            device_id=device,
            device_id_type=MESH,
        )
        copy.start()
        started.append(copy)
        return copy

    flows = [(0, 1), (0, -1), (1, 1), (1, -1)]
    bufs = [rowbuf, colbuf]
    ahead = [at_y, at_z]

    def chunk_of(sign, e):
        first = 0 if sign > 0 else 1
        return first if e % 2 == 0 else 1 - first

    def chunk(ref, c):
        return ref.at[pl.ds(c * HALF_BPD, HALF_BPD)]

    gathers = [[None] * events for _ in flows]

    def gather_send(e):
        for f, (axis, sign) in enumerate(flows):
            s, c = e // 2, chunk_of(sign, e)
            gathers[f][e] = send(
                chunk(bufs[axis][(-s * sign) % side], c),
                chunk(bufs[axis][(-(s + 1) * sign) % side], c),
                ag_send.at[f, e],
                ag_recv.at[f, e],
                ahead[axis](sign % side),
            )

    inflight = {}
    rows_x = BLK // (2 * xs)

    def dot_nt(a, b):
        return lax.dot_general(a, b, (((1,), (1,)), ((), ())), preferred_element_type=F32)

    def partial_scores(b):
        if b == 0:
            for k in range(BPD):
                s = dot_nt(emb[k], emb[k])
                part[b][:, :, k] = s.reshape(2, xs, rows_x, BLK)
            return
        for t, (ry, rz) in enumerate(plan[b - 1]):
            p = base[b - 1] + t
            first = jnp.maximum(tab[0, p], 0)
            second = jnp.maximum(tab[1, p], 0)
            s = dot_nt(rowbuf[ry][first], colbuf[rz][second])
            part[b][:, :, t] = s.reshape(2, xs, rows_x, BLK)

    def stage1(b):
        inflight[b] = [
            send(part[b].at[other], from_core[b], c1_send.at[b], c1_recv.at[b], at_core)
        ]

    def stage2(b):
        inflight[b][0].wait_recv()
        part[b][core] = part[b][core] + from_core[b][...]
        inflight[b] = [
            send(
                part[b].at[core, x_of(r)],
                from_x[b].at[r - 1],
                x2_send.at[b, r - 1],
                x2_recv.at[b, r - 1],
                at_x(r),
            )
            for r in range(1, xs)
        ]

    def stage3(b):
        for copy in inflight[b]:
            copy.wait_recv()
        total = part[b][core, x_here]
        for r in range(1, xs):
            total = total + from_x[b][r - 1]
        score[b][core, x_here] = total * scale
        mine = score[b].at[core, x_here]
        inflight[b] = [
            send(mine, mine, x3_send.at[b, r - 1], x3_recv.at[b, r - 1], at_x(r))
            for r in range(1, xs)
        ]

    def stage4(b):
        for copy in inflight[b]:
            copy.wait_recv()
        inflight[b] = [
            send(score[b].at[core], score[b].at[core], c4_send.at[b], c4_recv.at[b], at_core)
        ]

    def tile(b, t):
        return score[b][:, :, t].reshape(BLK, BLK)

    eye = lax.broadcasted_iota(jnp.int32, (BLK, BLK), 0) == lax.broadcasted_iota(
        jnp.int32, (BLK, BLK), 1
    )

    def stage5(b):
        inflight[b][0].wait_recv()
        if b == 0:

            def diag_body(t, carry):
                values = jnp.where(eye, NEG, tile(0, t))
                diag_stat[pl.ds(t, 1), :] = lse_rows(values)
                return carry

            lax.fori_loop(0, counts[0], diag_body, 0)
            return

        def body(t, carry):
            values = tile(b, t)
            col_stat[pl.ds(base[b - 1] + t, 1), :] = lse_rows(values)
            row_stat[pl.ds(base[b - 1] + t, 1), :] = lse_rows(values.T)
            return carry

        lax.fori_loop(0, counts[b], body, 0)

    stages = [stage1, stage2, stage3, stage4, stage5]
    progress = {}

    def tick():
        for b in sorted(progress):
            if progress[b] < len(stages):
                stages[progress[b]](b)
                progress[b] += 1

    gather_send(0)
    if events > 1:
        gather_send(1)
    partial_scores(0)
    progress[0] = 0
    tick()
    for e in range(events):
        for f in range(4):
            gathers[f][e].wait_recv()
        if e + 2 < events:
            gather_send(e + 2)
        b = half if e == events - 1 else ((e + 1) // 2 if e % 2 == 1 else 0)
        if b:
            partial_scores(b)
            progress[b] = 0
        tick()
    while any(p < len(stages) for p in progress.values()):
        tick()

    block_id = lax.broadcasted_iota(jnp.int32, (BPD, BLK), 0)
    for axis, stat in ((0, row_stat), (1, col_stat)):
        for r in range(side):
            found = []
            for o in range(side):
                if (r, o) == (0, 0):
                    continue
                p = pos[(r, o) if axis == 0 else (o, r)]
                line = jnp.broadcast_to(stat[pl.ds(p, 1), :], (BPD, BLK))
                found.append(jnp.where(block_id == tab[axis, p], line, NEG))
            stat_send[axis, r] = merge(found)
    exchanged = []
    for axis in (0, 1):
        for r in range(1, side):
            exchanged.append(
                send(
                    stat_send.at[axis, r],
                    stat_recv.at[axis, (-r) % side],
                    l_send.at[0, axis, r],
                    l_recv.at[0, axis, r],
                    ahead[axis](r),
                )
            )
    for copy in exchanged:
        copy.wait_recv()
    found = [diag_stat[...], stat_send[0, 0], stat_send[1, 0]]
    for axis in (0, 1):
        found += [stat_recv[axis, r] for r in range(1, side)]
    lse_own = merge(found)
    lse_out[...] = lse_own
    level[0, 0] = lse_own
    level[1, 0] = lse_own
    exchanged = []
    for axis in (0, 1):
        for r in range(1, side):
            exchanged.append(
                send(
                    level.at[axis, 0],
                    level.at[axis, (-r) % side],
                    l_send.at[1, axis, r],
                    l_recv.at[1, axis, r],
                    ahead[axis](r),
                )
            )
    for copy in exchanged:
        copy.wait_recv()

    def two_sided(values, li, lj):
        li = jnp.broadcast_to(li, (BLK, BLK)).T
        return jnp.exp(values - li) + jnp.exp(values - lj)

    def weights(b):
        def body(t, carry):
            p = base[b - 1] + t
            first, second = tab[0, p], tab[1, p]
            li = level[0, tab[2, p], pl.ds(jnp.maximum(first, 0), 1), :]
            lj = level[1, tab[3, p], pl.ds(jnp.maximum(second, 0), 1), :]
            w = jnp.where(first >= 0, two_sided(tile(b, t), li, lj), 0.0)
            w_ref[p] = w.astype(BF16)
            wt_ref[p] = w.T.astype(BF16)
            return carry

        lax.fori_loop(0, counts[b], body, 0)

    def contribution(axis, rel, c):
        slots = [o for o in range(side) if (rel, o) != (0, 0)]
        for i, o in enumerate(slots):
            p = pos[(rel, o) if axis == 0 else (o, rel)]
            mine, theirs = tab[axis, p], tab[1 - axis, p]
            lanes = pl.ds(i * BLK, BLK)
            stacked[lanes, :] = bufs[1 - axis][o][jnp.maximum(theirs, 0)]
            w = (w_ref if axis == 0 else wt_ref)[p]
            for k in range(HALF_BPD):
                wide[pl.ds(k * BLK, BLK), lanes] = jnp.where(
                    mine == c * HALF_BPD + k, w, jnp.zeros_like(w)
                )
        depth = pl.ds(0, len(slots) * BLK)
        return jnp.dot(wide[:, depth], stacked[depth, :], preferred_element_type=F32)

    shape = (HALF_BPD, BLK, emb.shape[2])
    scatters = [[None] * events for _ in flows]
    for e in range(events):
        rho = half - (e + 1) // 2
        if e == 0 or e % 2 == 1:
            weights(rho)
        for f, (axis, sign) in enumerate(flows):
            temp[f] = contribution(axis, (rho * sign) % side, chunk_of(sign, e)).reshape(shape)
        for f, (axis, sign) in enumerate(flows):
            if e < 2:
                out = fresh.at[f, e]
                out[...] = temp[f].astype(BF16)
            else:
                scatters[f][e - 2].wait_recv()
                out = ring_in[f][e - 2]
                out[...] = (temp[f] + out[...].astype(F32)).astype(BF16)
            scatters[f][e] = send(
                out, ring_in[f][e], rs_send.at[f, e], rs_recv.at[f, e], ahead[axis](sign % side)
            )

    for k in range(BPD):
        line = lse_own[k : k + 1]
        values = jnp.where(eye, NEG, tile(0, k))
        w = two_sided(values, line, line).astype(BF16)
        swap = lax.broadcasted_iota(jnp.int32, (BLK, BLK), 0) == partner[pl.ds(k, 1), :]
        swap = jnp.where(swap, 1.0, 0.0).astype(BF16)
        acc[k] = jnp.dot(w, emb[k], preferred_element_type=F32) - 2.0 * jnp.dot(
            swap, emb[k], preferred_element_type=F32
        )
    for axis in (0, 1):
        for c in (0, 1):
            rows = pl.ds(c * HALF_BPD, HALF_BPD)
            acc[rows] = acc[rows] + contribution(axis, 0, c).reshape(shape)
    last = [e for e in range(events) if half - (e + 1) // 2 == 1]
    for e in last:
        for f, (axis, sign) in enumerate(flows):
            scatters[f][e].wait_recv()
            rows = pl.ds(chunk_of(sign, e) * HALF_BPD, HALF_BPD)
            acc[rows] = acc[rows] + ring_in[f][e][...].astype(F32)
    grad_out[...] = acc[...].astype(BF16)
    for copy in started:
        copy.wait_send()


def fused(embeddings, tab, partner, side, xs):
    _, _, width = embeddings.shape
    half = side // 2
    plan = slot_plan(side)
    counts = [BPD] + [len(batch) for batch in plan]
    nb = len(counts)
    nslot = sum(counts[1:])
    events = 2 * half - 1
    rows_x = BLK // (2 * xs)
    dma = pltpu.SemaphoreType.DMA
    blocks = pltpu.VMEM((BPD, BLK, width), BF16)
    chunk = pltpu.VMEM((HALF_BPD, BLK, width), BF16)
    stats = pltpu.VMEM((2, side, BPD, BLK), F32)
    scratch = [blocks] * (2 * (side - 1))
    scratch += [pltpu.VMEM((2, xs, n, rows_x, BLK), F32) for n in counts]
    scratch += [pltpu.VMEM((xs, n, rows_x, BLK), F32) for n in counts]
    scratch += [pltpu.VMEM((max(xs - 1, 1), n, rows_x, BLK), F32) for n in counts]
    scratch += [pltpu.VMEM((2, xs, n, rows_x, BLK), F32) for n in counts]
    padded = -(-nslot // 8) * 8
    scratch += [pltpu.VMEM((padded, BLK), F32)] * 2 + [pltpu.VMEM((BPD, BLK), F32)]
    scratch += [stats] * 3 + [pltpu.VMEM((nslot, BLK, BLK), BF16)] * 2
    scratch += [
        pltpu.VMEM((HALF_BPD * BLK, side * BLK), BF16),
        pltpu.VMEM((side * BLK, width), BF16),
        pltpu.VMEM((4, HALF_BPD, BLK, width), F32),
        pltpu.VMEM((BPD, BLK, width), F32),
        pltpu.VMEM((4, 2, HALF_BPD, BLK, width), BF16),
    ]
    scratch += [chunk] * (4 * events)
    scratch += [dma((4, events))] * 2 + [dma((nb,))] * 2 + [dma((nb, max(xs - 1, 1)))] * 4
    scratch += [dma((nb,))] * 2 + [dma((2, 2, side))] * 2 + [dma((4, events))] * 2
    vmem = pl.BlockSpec(memory_space=pltpu.VMEM)
    flops = 2 * BLK * BLK * width * (counts[0] * 4 + nslot * (1 + 2 * BPD))
    return pl.pallas_call(
        functools.partial(kernel, side, xs, 2.0 / math.sqrt(D)),
        out_shape=(
            jax.ShapeDtypeStruct((BPD, BLK), F32),
            jax.ShapeDtypeStruct((BPD, BLK, width), BF16),
        ),
        in_specs=[vmem, pl.BlockSpec(memory_space=pltpu.SMEM), vmem],
        out_specs=(vmem, vmem),
        scratch_shapes=scratch,
        compiler_params=pltpu.CompilerParams(
            collective_id=0, has_side_effects=True, vmem_limit_bytes=VMEM_BYTES
        ),
        cost_estimate=pl.CostEstimate(
            flops=flops, bytes_accessed=4 * embeddings.size, transcendentals=6 * nslot * BLK * BLK
        ),
    )(embeddings, tab, partner)


def per_device(embeddings, pairs, partner):
    rows_here, width = embeddings.shape
    side = math.isqrt(lax.axis_size("tensor"))
    xs = lax.axis_size("dp") // 2
    tab = slot_tables(pairs, lax.axis_index("tensor"), side)
    lse, grad = fused(
        embeddings.reshape(BPD, BLK, width),
        tab,
        (partner % BLK).reshape(BPD, BLK),
        side,
        xs,
    )
    return lse.reshape(rows_here), grad.reshape(rows_here, width)


def solution(mesh):
    in_specs = (P("tensor", "dp"), P(), P("tensor"))
    out_specs = (P("tensor"), P("tensor", "dp"))
    return jax.shard_map(
        per_device, mesh=mesh, in_specs=in_specs, out_specs=out_specs, check_vma=False
    )
```

time: 581 us -> 241 us (0.41)
  waiting for transfers between devices: 427 us -> 0 us
  Pallas kernels: 0 us -> 232 us
  matrix products: 41 us -> 0 us
  blocking collectives: 36.4 us -> 0 us
  local copies, waits for them, and re-layouts: 33.1 us -> 5.86 us
  starting transfers between devices: 13.8 us -> 0 us
  between operations: 14.1 us -> 0.75 us
  other arithmetic: 15.1 us -> 2.66 us
    pallas_call x0 -> x1, Pallas kernels: none -> 232 us  [fused(): pl.pallas_call(functools.partial(kernel, side, xs, 2.0 / math.sqrt(D)), o...]
    all_gather x2 -> x0, waiting for transfers between devices: 172 us -> none  [the longest x1 90.1 us: per_device(): row_blocks = lax.all_gather(own_blocks, 'tensor', axis_index_groups=along_y)]
    reduce_scatter x2 -> x0, waiting for transfers between devices: 160 us -> none  [the longest x1 88.1 us: per_device(): row_grad = lax.psum_scatter(row_terms, 'tensor', axis_index_groups=along_y)]
    psum x1 -> x0, waiting for transfers between devices: 81.4 us -> none  [per_device(): diag_summed, pair_summed = lax.psum((diag_partial, pair_partial), 'dp')]
    dot_general x5 -> x0, matrix products: 41 us -> none  [the longest x1 14.4 us: per_device(): jnp.einsum('yzkij,yziw->zkjw', wide_col, first_rows, preferred_element_ty...]
    all_gather x2 -> x0, blocking collectives: 36.4 us -> none  [the longest x1 18.3 us: per_device(): row_lse = lax.all_gather(lse_own, 'tensor', axis_index_groups=along_y)]
    gather x5 -> x1, local copies, waits for them, and re-layouts: 21.1 us -> 0.66 us  [slot_tables(): source = rows[(y_here + ry) % side]]
    all_to_all x2 -> x0, starting transfers between devices: 13.6 us -> none  [the longest x1 7.1 us: per_device(): lax.all_to_all(col_stats, 'tensor', 0, 0, axis_index_groups=along_z, tile...]
  transfers between devices with their start and end apart: 7 -> 0, of which waited for: 7 -> 0; matrix products, arithmetic and copies ran while one was open for 6% -> 0% of each run, Pallas kernels for 0% -> 0%
where the time goes in v2:
time: 241 us
  Pallas kernels  232 us (96%)
  local copies, waits for them, and re-layouts  5.86 us (2%)
  other arithmetic  2.66 us (1%)
    pallas_call x1, Pallas kernels, fused(): pl.pallas_call(functools.partial(kernel, side, xs, 2.0 / math.sqrt(D)), o...  232 us

profile of v2, /device:TPU:1, one launch (start us, length us, event | category | flops | bytes accessed | tf_op | source)
XLA Modules:
  0.0 241.1 jit_solution(7234856598075149619)
XLA Ops:
  0.7 0.7 compare_select_fusion
  1.4 1.3 fusion.10.refs_2_
  2.6 0.8 reshape.47
  3.5 0.0 copy-start.2
  3.5 0.0 copy-start.3
  3.5 0.0 copy-start
  3.6 0.7 gather_fusion
  4.2 0.1 fusion.16
  4.3 0.1 copy.23
  4.3 0.1 copy.24
  4.4 0.1 fusion.3
  4.5 0.0 copy-done.2
  4.5 0.0 copy-done.3
  4.5 0.6 pad_add_fusion.refs_1_
  5.1 0.0 copy-done
  5.1 1.3 copy.21
  6.4 231.8 %shard_map.68 = (f32[8,128]{1,0:T(8,128)}, bf16[8,128,448]{2,1,0:T(8,128)(2,1)}) custom-call(bf16[8,128,448]{2,1,0:T(8,128)(2,1)} %bitcast.47, s32[4,63]{1,0:T(4,128)} %pad_add_fusion.refs_1_, s32[8,128]{1,0:T(8,128)} %fusion.10.refs_2_), custom_call_target="tpu_custom_call" | custom-call | flops 16192110592 | bytes 1835008 | tf_op jit(solution)/shard_map/pallas_call | solution.py:436
  238.3 0.0 copy-start.1
  238.3 2.2 copy.25
  240.5 0.0 copy-done.1
  240.5 0.6 copy.30
  (5 shorter events, 0.1 us)
Async XLA Ops:
  3.5 1.0 copy-start.2
  3.5 1.0 copy-start.3
  3.5 1.6 copy-start
  238.3 2.2 copy-start.1

commit v3 on v2

v3 whole, which is shorter than its diff:
```python
import functools
import math

import jax
import jax.numpy as jnp
import numpy as np
from jax import lax
from jax.experimental import pallas as pl
from jax.experimental.pallas import tpu as pltpu
from jax.sharding import PartitionSpec as P

D = 3584
BPD = 8
BLK = 128
HALF_BPD = BPD // 2
NEG = -1e30
VMEM_BYTES = 63 * 1024 * 1024
MESH = pl.DeviceIdType.MESH
F32 = jnp.float32
BF16 = jnp.bfloat16


def ring_distance(rel, side):
    return min(rel, side - rel)


def slot_plan(side):
    batches = []
    for step in range(1, side // 2 + 1):
        batches.append(
            [
                (ry, rz)
                for ry in range(side)
                for rz in range(side)
                if max(ring_distance(ry, side), ring_distance(rz, side)) == step
            ]
        )
    return batches


def slot_grid(side):
    order = [slot for batch in slot_plan(side) for slot in batch]
    grid = np.zeros((-(-len(order) // 8) * 8, BLK), np.int32)
    grid[: len(order), :2] = order
    return grid


def lse_rows(values):
    top = jnp.max(values, axis=0, keepdims=True)
    return top + jnp.log(jnp.sum(jnp.exp(values - top), axis=0, keepdims=True))


def merge(parts):
    top = functools.reduce(jnp.maximum, parts)
    return top + jnp.log(functools.reduce(jnp.add, [jnp.exp(p - top) for p in parts]))


def kernel(side, xs, scale, *refs):
    half = side // 2
    plan = slot_plan(side)
    counts = [BPD] + [len(batch) for batch in plan]
    nb = len(counts)
    pos = {slot: i for i, slot in enumerate(s for batch in plan for s in batch)}
    base = [0]
    for batch in plan:
        base.append(base[-1] + len(batch))
    events = 2 * half - 1

    refs = list(refs)

    def take(n):
        out = refs[:n]
        del refs[:n]
        return out

    emb, pairs, partner, grid, lse_out, grad_out = take(6)
    (own,) = take(1)
    rowbuf = [own] + take(side - 1)
    colbuf = [own] + take(side - 1)
    part = take(nb)
    from_core = take(nb)
    from_x = take(nb)
    score = take(nb)
    (row_stat, col_stat, diag_stat, stat_send, stat_recv, level, w_ref, wt_ref) = take(8)
    (keys, dp_stat) = take(2)
    (wide, stacked, temp, acc, fresh, done, tab_vmem, tab) = take(8)
    ring_in = [take(events) for _ in range(4)]
    (ag_send, ag_recv, c1_send, c1_recv) = take(4)
    x_sems = take(2)
    (c4_send, c4_recv, l_send, l_recv, rs_send, rs_recv, in_sem, out_sem, tab_sem) = take(9)
    dp_sems = take(2)

    me = lax.axis_index("tensor")
    d = lax.axis_index("dp")
    z_here, y_here = lax.div(me, side), lax.rem(me, side)
    x_here, core = lax.div(d, 2), lax.rem(d, 2)
    other = 1 - core

    def at_y(r):
        return {"dp": d, "tensor": z_here * side + lax.rem(y_here + r, side)}

    def at_z(r):
        return {"dp": d, "tensor": lax.rem(z_here + r, side) * side + y_here}

    def x_of(r):
        return lax.rem(x_here + r + xs, xs)

    def at_x(r):
        return {"dp": x_of(r) * 2 + core, "tensor": me}

    def at_dp(r):
        return {"dp": lax.rem(d + r, 2 * xs), "tensor": me}

    at_core = {"dp": x_here * 2 + other, "tensor": me}
    peers = [at_y(r) for r in range(1, side)] + [at_z(r) for r in range(1, side)]
    peers += [at_dp(r) for r in range(1, 2 * xs)]
    loads = [
        pltpu.make_async_copy(emb.at[:, pl.ds(k * BLK, BLK)], own.at[k], in_sem.at[k])
        for k in range(BPD)
    ]
    for copy in loads:
        copy.start()
    barrier = pltpu.get_barrier_semaphore()
    for peer in peers:
        pl.semaphore_signal(barrier, inc=1, device_id=peer, device_id_type=MESH)
    for copy in loads:
        copy.wait()
    pl.semaphore_wait(barrier, len(peers))

    started = []

    def send(src, dst, send_sem, recv_sem, device):
        copy = pltpu.make_async_remote_copy(
            src_ref=src,
            dst_ref=dst,
            send_sem=send_sem,
            recv_sem=recv_sem,
            device_id=device,
            device_id_type=MESH,
        )
        copy.start()
        started.append(copy)
        return copy

    flows = [(0, 1), (0, -1), (1, 1), (1, -1)]
    bufs = [rowbuf, colbuf]
    ahead = [at_y, at_z]

    def chunk_of(sign, e):
        first = 0 if sign > 0 else 1
        return first if e % 2 == 0 else 1 - first

    def chunk(ref, c):
        return ref.at[pl.ds(c * HALF_BPD, HALF_BPD)]

    gathers = [[None] * events for _ in flows]

    def gather_send(e):
        for f, (axis, sign) in enumerate(flows):
            s, c = e // 2, chunk_of(sign, e)
            gathers[f][e] = send(
                chunk(bufs[axis][(-s * sign) % side], c),
                chunk(bufs[axis][(-(s + 1) * sign) % side], c),
                ag_send.at[f, e],
                ag_recv.at[f, e],
                ahead[axis](sign % side),
            )

    inflight = {}
    rows_x = BLK // (2 * xs)
    per_line = BLK // rows_x
    group0 = [0, 0]
    for n in counts[1:]:
        group0.append(group0[-1] + -(-n // per_line))

    def dot_tn(a, b):
        return lax.dot_general(a, b, (((0,), (0,)), ((), ())), preferred_element_type=F32)

    def slot_tables():
        ry, rz = grid[:, 0:1], grid[:, 1:2]
        source = z_here * side + lax.rem(y_here + ry, side)
        wanted = lax.rem(z_here + rz, side) * side + y_here
        npair = pairs.shape[1]
        per_group = npair // (side * side)
        lane = lax.broadcasted_iota(jnp.int32, (grid.shape[0], npair), 1)
        low = source * per_group
        match = (lane >= low) & (lane < low + per_group)
        match = match & (lax.shift_right_logical(pairs[1:2, :], 3) == wanted)
        first = jnp.max(jnp.where(match, pairs[0:1, :] & 7, -1), axis=1, keepdims=True)
        second = jnp.max(jnp.where(match, pairs[1:2, :] & 7, -1), axis=1, keepdims=True)
        column = lax.broadcasted_iota(jnp.int32, (grid.shape[0], BLK), 1)
        tab_vmem[...] = jnp.where(
            column == 0, first, jnp.where(column == 1, second, jnp.where(column == 2, ry, rz))
        )
        copy = pltpu.make_async_copy(tab_vmem, tab, tab_sem)
        copy.start()
        copy.wait()
        lane_tile = lax.broadcasted_iota(jnp.int32, (1, BLK), 1) // rows_x
        for b in range(1, nb):
            for t in range(counts[b]):
                p = base[b - 1] + t
                first = tab[p, 0]
                key = jnp.where(first >= 0, first + BPD * tab[p, 2], -1)
                line = pl.ds(group0[b] + t // per_line, 1)
                held = jnp.full((1, BLK), -1, jnp.int32) if t % per_line == 0 else keys[line, :]
                keys[line, :] = jnp.where(lane_tile == t % per_line, key, held)

    def partial_scores(b):
        if b == 0:
            for k in range(BPD):
                s = dot_tn(own[k], own[k])
                part[b][:, :, k] = s.reshape(2, xs, rows_x, BLK)
            return
        for t, (ry, rz) in enumerate(plan[b - 1]):
            p = base[b - 1] + t
            first = jnp.maximum(tab[p, 0], 0)
            second = jnp.maximum(tab[p, 1], 0)
            s = dot_tn(rowbuf[ry][first], colbuf[rz][second])
            part[b][:, :, t] = s.reshape(2, xs, rows_x, BLK)

    def stage1(b):
        inflight[b] = [
            send(part[b].at[other], from_core[b], c1_send.at[b], c1_recv.at[b], at_core)
        ]

    def x_send(b, i, src, dst, r):
        return send(src, dst, x_sems[0].at[b, i], x_sems[1].at[b, i], at_x(r))

    def stage2(b):
        inflight[b][0].wait_recv()
        part[b][core] = part[b][core] + from_core[b][...]
        inflight[b] = [
            x_send(b, r, part[b].at[core, x_of(r)], from_x[b].at[r - 1], r) for r in range(1, xs)
        ]

    def reduce_rows(b):
        for copy in inflight[b]:
            copy.wait_recv()
        total = part[b][core, x_here]
        for r in range(1, xs):
            total = total + from_x[b][r - 1]
        score[b][core, x_here] = total * scale

    def spread_rows(b):
        mine = score[b].at[core, x_here]
        inflight[b] = [x_send(b, xs + r, mine, mine, r) for r in range(1, xs)]

    def row_partials(b):
        mine = score[b][core, x_here]
        n = counts[b]
        if b == 0:
            row = lax.broadcasted_iota(jnp.int32, mine.shape, 1) + (core * xs + x_here) * rows_x
            values = jnp.where(row == lax.broadcasted_iota(jnp.int32, mine.shape, 2), NEG, mine)
        else:
            values = mine
        top = jnp.max(values, axis=1, keepdims=True)
        total = jnp.sum(jnp.exp(values - top), axis=1, keepdims=True)
        cols = (top + jnp.log(total)).reshape(n, BLK)
        if b == 0:
            diag_stat[...] = cols
            return
        col_stat[pl.ds(base[b - 1], n), :] = cols
        flat = mine.reshape(n * rows_x, BLK)
        for g in range(-(-n // per_line)):
            lines = flat[g * BLK : (g + 1) * BLK]
            if lines.shape[0] < BLK:
                lines = jnp.concatenate([lines, jnp.zeros((BLK - lines.shape[0], BLK), F32)], axis=0)
            row_stat[pl.ds(group0[b] + g, 1), :] = lse_rows(lines.T)

    def stage3(b):
        reduce_rows(b)
        spread_rows(b)
        row_partials(b)

    def stage4(b):
        for copy in inflight[b]:
            copy.wait_recv()
        inflight[b] = [
            send(score[b].at[core], score[b].at[core], c4_send.at[b], c4_recv.at[b], at_core)
        ]

    def stage5(b):
        inflight[b][0].wait_recv()

    def tile(b, t):
        return score[b][:, :, t].reshape(BLK, BLK)

    eye = lax.broadcasted_iota(jnp.int32, (BLK, BLK), 0) == lax.broadcasted_iota(
        jnp.int32, (BLK, BLK), 1
    )

    stages = [stage1, stage2, stage3, stage4, stage5]
    progress = {}

    def tick():
        for b in sorted(progress):
            if progress[b] < len(stages):
                stages[progress[b]](b)
                progress[b] += 1

    gather_send(0)
    if events > 1:
        gather_send(1)
    partial_scores(0)
    progress[0] = 0
    tick()
    slot_tables()
    tick()
    for e in range(events):
        for f in range(4):
            gathers[f][e].wait_recv()
        if e + 2 < events:
            gather_send(e + 2)
        b = half if e == events - 1 else ((e + 1) // 2 if e % 2 == 1 else 0)
        if b:
            partial_scores(b)
            if b >= half - 1:
                stage1(b)
                stage2(b)
            else:
                progress[b] = 0
        tick()
        tick()
    while any(p < len(stages) for p in progress.values()):
        tick()
    tail = [b for b in (half - 1, half) if b >= 1]
    for b in tail:
        reduce_rows(b)
        if b == half:
            for late in reversed(tail):
                spread_rows(late)
        row_partials(b)

    block_id = lax.broadcasted_iota(jnp.int32, (BPD, BLK), 0)

    def over_lanes(values, combine):
        shift = BLK // 2
        while shift >= rows_x:
            values = combine(values, pltpu.roll(values, shift, 1))
            shift //= 2
        return values

    def exchange(step, axis, source, slots):
        return [
            send(
                source(r),
                slots.at[axis, (-r) % side],
                l_send.at[step, axis, r],
                l_recv.at[step, axis, r],
                ahead[axis](r),
            )
            for r in range(1, side)
        ]

    for r in range(side):
        found = []
        for o in range(side):
            if (r, o) == (0, 0):
                continue
            p = pos[(o, r)]
            line = jnp.broadcast_to(col_stat[pl.ds(p, 1), :], (BPD, BLK))
            found.append(jnp.where(block_id == tab[p, 1], line, NEG))
        stat_send[1, r] = merge(found)
    exchanged = exchange(0, 1, lambda r: stat_send.at[1, r], stat_recv)
    for r in range(side):
        found = []
        for g in range(group0[-1]):
            line = jnp.broadcast_to(row_stat[pl.ds(g, 1), :], (BPD, BLK))
            key = jnp.broadcast_to(keys[pl.ds(g, 1), :], (BPD, BLK))
            found.append(jnp.where(key == block_id + BPD * r, line, NEG))
        top = over_lanes(functools.reduce(jnp.maximum, found), jnp.maximum)
        total = functools.reduce(jnp.add, [jnp.exp(v - top) for v in found])
        stat_send[0, r] = top + jnp.log(over_lanes(total, jnp.add))
    exchanged += exchange(0, 0, lambda r: stat_send.at[0, r], stat_recv)
    for copy in exchanged:
        copy.wait_recv()
    dp_stat[0, 0] = merge([stat_send[0, 0]] + [stat_recv[0, r] for r in range(1, side)])
    dp_stat[0, 1] = merge(
        [diag_stat[...], stat_send[1, 0]] + [stat_recv[1, r] for r in range(1, side)]
    )
    exchanged = [
        send(
            dp_stat.at[0],
            dp_stat.at[2 * xs - r],
            dp_sems[0].at[r],
            dp_sems[1].at[r],
            at_dp(r),
        )
        for r in range(1, 2 * xs)
    ]
    for copy in exchanged:
        copy.wait_recv()
    lane_group = lax.broadcasted_iota(jnp.int32, (BPD, BLK), 1) // rows_x
    found = []
    for r in range(2 * xs):
        source = lax.rem(d + r, 2 * xs)
        part_of = lax.rem(source, 2) * xs + lax.div(source, 2)
        found.append(jnp.where(lane_group == part_of, dp_stat[r, 0], NEG))
        found.append(dp_stat[r, 1])
    lse_own = merge(found)
    lse_out[...] = lse_own
    level[0, 0] = lse_own
    level[1, 0] = lse_own
    exchanged = exchange(1, 0, lambda r: level.at[0, 0], level)
    exchanged += exchange(1, 1, lambda r: level.at[1, 0], level)
    for stage in (stage4, stage5):
        for b in reversed(tail):
            stage(b)
    for copy in exchanged:
        copy.wait_recv()

    def two_sided(values, li, lj):
        li = jnp.broadcast_to(li, (BLK, BLK)).T
        return jnp.exp(values - li) + jnp.exp(values - lj)

    def weights(b):
        def body(t, carry):
            p = base[b - 1] + t
            first, second = tab[p, 0], tab[p, 1]
            li = level[0, tab[p, 2], pl.ds(jnp.maximum(first, 0), 1), :]
            lj = level[1, tab[p, 3], pl.ds(jnp.maximum(second, 0), 1), :]
            w = jnp.where(first >= 0, two_sided(tile(b, t), li, lj), 0.0)
            w_ref[p] = w.astype(BF16)
            wt_ref[p] = w.T.astype(BF16)
            return carry

        lax.fori_loop(0, counts[b], body, 0)

    def contribution(axis, rel, c):
        slots = [o for o in range(side) if (rel, o) != (0, 0)]
        for i, o in enumerate(slots):
            p = pos[(rel, o) if axis == 0 else (o, rel)]
            mine, theirs = tab[p, axis], tab[p, 1 - axis]
            lanes = pl.ds(i * BLK, BLK)
            stacked[:, lanes] = bufs[1 - axis][o][jnp.maximum(theirs, 0)]
            w = (wt_ref if axis == 0 else w_ref)[p]
            for k in range(HALF_BPD):
                wide[lanes, pl.ds(k * BLK, BLK)] = jnp.where(
                    mine == c * HALF_BPD + k, w, jnp.zeros_like(w)
                )
        depth = pl.ds(0, len(slots) * BLK)
        return jnp.dot(stacked[:, depth], wide[depth, :], preferred_element_type=F32)

    def by_block(out, offset, values):
        for k in range(HALF_BPD):
            out[offset + k] = values[:, k * BLK : (k + 1) * BLK]

    scatters = [[None] * events for _ in flows]
    for e in range(events):
        rho = half - (e + 1) // 2
        if e == 0 or e % 2 == 1:
            weights(rho)
        for f, (axis, sign) in enumerate(flows):
            by_block(temp.at[f], 0, contribution(axis, (rho * sign) % side, chunk_of(sign, e)))
        for f, (axis, sign) in enumerate(flows):
            if e < 2:
                out = fresh.at[f, e]
                out[...] = temp[f].astype(BF16)
            else:
                scatters[f][e - 2].wait_recv()
                out = ring_in[f][e - 2]
                out[...] = (temp[f] + out[...].astype(F32)).astype(BF16)
            scatters[f][e] = send(
                out, ring_in[f][e], rs_send.at[f, e], rs_recv.at[f, e], ahead[axis](sign % side)
            )

    for k in range(BPD):
        line = lse_own[k : k + 1]
        values = jnp.where(eye, NEG, tile(0, k))
        w = two_sided(values, line, line).T.astype(BF16)
        swap = lax.broadcasted_iota(jnp.int32, (BLK, BLK), 0) == partner[pl.ds(k, 1), :]
        swap = jnp.where(swap, 1.0, 0.0).astype(BF16)
        acc[k] = jnp.dot(own[k], w, preferred_element_type=F32) - 2.0 * jnp.dot(
            own[k], swap, preferred_element_type=F32
        )
    for axis in (0, 1):
        for c in (0, 1):
            rows = pl.ds(c * HALF_BPD, HALF_BPD)
            by_block(temp.at[0], 0, contribution(axis, 0, c))
            acc[rows] = acc[rows] + temp[0]
    last = [e for e in range(events) if half - (e + 1) // 2 == 1]
    for e in last:
        for f, (axis, sign) in enumerate(flows):
            scatters[f][e].wait_recv()
            rows = pl.ds(chunk_of(sign, e) * HALF_BPD, HALF_BPD)
            acc[rows] = acc[rows] + ring_in[f][e][...].astype(F32)
    stores = []
    for k in range(BPD):
        done[k] = acc[k].astype(BF16)
        stores.append(
            pltpu.make_async_copy(done.at[k], grad_out.at[:, pl.ds(k * BLK, BLK)], out_sem.at[k])
        )
        stores[k].start()
    for copy in stores:
        copy.wait()
    for copy in started:
        copy.wait_send()


def fused(embeddings, pairs, partner, side, xs):
    width = embeddings.shape[0]
    half = side // 2
    plan = slot_plan(side)
    counts = [BPD] + [len(batch) for batch in plan]
    nb = len(counts)
    nslot = sum(counts[1:])
    events = 2 * half - 1
    rows_x = BLK // (2 * xs)
    dma = pltpu.SemaphoreType.DMA
    blocks = pltpu.VMEM((BPD, width, BLK), BF16)
    chunk = pltpu.VMEM((HALF_BPD, width, BLK), BF16)
    stats = pltpu.VMEM((2, side, BPD, BLK), F32)
    scratch = [blocks] * (2 * side - 1)
    scratch += [pltpu.VMEM((2, xs, n, rows_x, BLK), F32) for n in counts]
    scratch += [pltpu.VMEM((xs, n, rows_x, BLK), F32) for n in counts]
    scratch += [pltpu.VMEM((xs - 1, n, rows_x, BLK), F32) for n in counts]
    scratch += [pltpu.VMEM((2, xs, n, rows_x, BLK), F32) for n in counts]
    padded = -(-nslot // 8) * 8
    scratch += [pltpu.VMEM((padded, BLK), F32)] * 2 + [pltpu.VMEM((BPD, BLK), F32)]
    scratch += [stats] * 3 + [pltpu.VMEM((nslot, BLK, BLK), BF16)] * 2
    scratch += [pltpu.VMEM((padded, BLK), jnp.int32), pltpu.VMEM((2 * xs, 2, BPD, BLK), F32)]
    scratch += [
        pltpu.VMEM((side * BLK, HALF_BPD * BLK), BF16),
        pltpu.VMEM((width, side * BLK), BF16),
        pltpu.VMEM((4, HALF_BPD, width, BLK), F32),
        pltpu.VMEM((BPD, width, BLK), F32),
        pltpu.VMEM((4, 2, HALF_BPD, width, BLK), BF16),
        blocks,
        pltpu.VMEM((padded, BLK), jnp.int32),
        pltpu.SMEM((padded, BLK), jnp.int32),
    ]
    scratch += [chunk] * (4 * events)
    scratch += [dma((4, events))] * 2 + [dma((nb,))] * 2 + [dma((nb, 2 * xs))] * 2
    scratch += [dma((nb,))] * 2 + [dma((2, 2, side))] * 2 + [dma((4, events))] * 2
    scratch += [dma((BPD,))] * 2 + [dma(())] + [dma((2 * xs,))] * 2
    anywhere = pl.BlockSpec(memory_space=pl.ANY)
    vmem = pl.BlockSpec(memory_space=pltpu.VMEM)
    flops = 2 * BLK * BLK * width * (counts[0] * 4 + nslot * (1 + 2 * BPD))
    return pl.pallas_call(
        functools.partial(kernel, side, xs, 2.0 / math.sqrt(D)),
        out_shape=(
            jax.ShapeDtypeStruct((BPD, BLK), F32),
            jax.ShapeDtypeStruct((width, BPD * BLK), BF16),
        ),
        in_specs=[anywhere, vmem, vmem, vmem],
        out_specs=(vmem, anywhere),
        scratch_shapes=scratch,
        compiler_params=pltpu.CompilerParams(
            collective_id=0, has_side_effects=True, vmem_limit_bytes=VMEM_BYTES
        ),
        cost_estimate=pl.CostEstimate(
            flops=flops, bytes_accessed=4 * embeddings.size, transcendentals=6 * nslot * BLK * BLK
        ),
    )(embeddings, pairs, partner, jnp.asarray(slot_grid(side)))


def per_device(embeddings, pairs, partner):
    rows_here, width = embeddings.shape
    side = math.isqrt(lax.axis_size("tensor"))
    xs = lax.axis_size("dp") // 2
    lse, grad = fused(
        embeddings.T, pairs.T, (partner % BLK).reshape(BPD, BLK), side, xs
    )
    return lse.reshape(rows_here), grad.T


def solution(mesh):
    in_specs = (P("tensor", "dp"), P(), P("tensor"))
    out_specs = (P("tensor"), P("tensor", "dp"))
    return jax.shard_map(
        per_device, mesh=mesh, in_specs=in_specs, out_specs=out_specs, check_vma=False
    )
```

time: 241 us -> 204 us (0.85)
  Pallas kernels: 232 us -> 199 us
  local copies, waits for them, and re-layouts: 5.86 us -> 3.42 us
    pallas_call x1, Pallas kernels: 232 us -> 199 us  [fused(): pl.pallas_call(functools.partial(kernel, side, xs, 2.0 / math.sqrt(D)), o...]
where the time goes in v3:
time: 204 us
  Pallas kernels  199 us (98%)
  local copies, waits for them, and re-layouts  3.42 us (2%)
    pallas_call x1, Pallas kernels, fused(): pl.pallas_call(functools.partial(kernel, side, xs, 2.0 / math.sqrt(D)), o...  199 us

profile of v3, /device:TPU:1, one launch (start us, length us, event | category | flops | bytes accessed | tf_op | source)
XLA Modules:
  0.0 204.0 jit_solution(1871657760799668918)
XLA Ops:
  0.6 1.3 fusion.1.refs_2_
  1.9 198.7 %shard_map.59 = (f32[8,128]{1,0:T(8,128)}, bf16[448,1024]{1,0:T(8,128)(2,1)}) custom-call(bf16[448,1024]{1,0:T(8,128)(2,1)} %bitcast.8, s32[2,3072]{1,0:T(2,128)} %bitcast.9, s32[8,128]{1,0:T(8,128)} %fusion.1.refs_2_, s32[64,128]{1,0:T(8,128)} %constant.17.clone.refs_3_), custom_call_target="tpu_custom_call" | custom-call | flops 16192110592 | bytes 1835008 | tf_op jit(solution)/shard_map/pallas_call | solution.py:539
  200.6 0.0 copy-start
  200.6 0.7 copy-done
  201.3 0.6 copy.8
  201.8 2.2 %copy.9 = bf16[1024,448]{0,1:T(8,128)(2,1)} copy(bf16[1024,448]{0,1:T(8,128)(2,1)} %bitcast.6) | data formatting | bytes 1835008
Async XLA Ops:
  200.6 0.7 copy-start

commit v4 on v3

--- a/solution.py
+++ b/solution.py
@@ -27,14 +27,13 @@
 def slot_plan(side):
     batches = []
     for step in range(1, side // 2 + 1):
-        batches.append(
-            [
-                (ry, rz)
-                for ry in range(side)
-                for rz in range(side)
-                if max(ring_distance(ry, side), ring_distance(rz, side)) == step
-            ]
-        )
+        batch = [
+            (ry, rz)
+            for ry in range(side)
+            for rz in range(side)
+            if max(ring_distance(ry, side), ring_distance(rz, side)) == step
+        ]
+        batches.append(sorted(batch, key=lambda slot: slot[0] != side // 2))
     return batches
 
 
@@ -155,16 +154,16 @@
 
     gathers = [[None] * events for _ in flows]
 
-    def gather_send(e):
-        for f, (axis, sign) in enumerate(flows):
-            s, c = e // 2, chunk_of(sign, e)
-            gathers[f][e] = send(
-                chunk(bufs[axis][(-s * sign) % side], c),
-                chunk(bufs[axis][(-(s + 1) * sign) % side], c),
-                ag_send.at[f, e],
-                ag_recv.at[f, e],
-                ahead[axis](sign % side),
-            )
+    def gather_send(f, e):
+        axis, sign = flows[f]
+        s, c = e // 2, chunk_of(sign, e)
+        gathers[f][e] = send(
+            chunk(bufs[axis][(-s * sign) % side], c),
+            chunk(bufs[axis][(-(s + 1) * sign) % side], c),
+            ag_send.at[f, e],
+            ag_recv.at[f, e],
+            ahead[axis](sign % side),
+        )
 
     inflight = {}
     rows_x = BLK // (2 * xs)
@@ -298,9 +297,9 @@
                 stages[progress[b]](b)
                 progress[b] += 1
 
-    gather_send(0)
-    if events > 1:
-        gather_send(1)
+    for e in range(min(2, events)):
+        for f in range(4):
+            gather_send(f, e)
     partial_scores(0)
     progress[0] = 0
     tick()
@@ -309,8 +308,8 @@
     for e in range(events):
         for f in range(4):
             gathers[f][e].wait_recv()
-        if e + 2 < events:
-            gather_send(e + 2)
+            if e + 2 < events:
+                gather_send(f, e + 2)
         b = half if e == events - 1 else ((e + 1) // 2 if e % 2 == 1 else 0)
         if b:
             partial_scores(b)
@@ -324,13 +323,6 @@
     while any(p < len(stages) for p in progress.values()):
         tick()
     tail = [b for b in (half - 1, half) if b >= 1]
-    for b in tail:
-        reduce_rows(b)
-        if b == half:
-            for late in reversed(tail):
-                spread_rows(late)
-        row_partials(b)
-
     block_id = lax.broadcasted_iota(jnp.int32, (BPD, BLK), 0)
 
     def over_lanes(values, combine):
@@ -339,6 +331,43 @@
             values = combine(values, pltpu.roll(values, shift, 1))
             shift //= 2
         return values
+
+    def col_merge(r, b_from, b_to, more):
+        found = list(more)
+        for o in range(side):
+            if (o, r) in pos and base[b_from] <= pos[(o, r)] < base[b_to]:
+                p = pos[(o, r)]
+                line = jnp.broadcast_to(col_stat[pl.ds(p, 1), :], (BPD, BLK))
+                found.append(jnp.where(block_id == tab[p, 1], line, NEG))
+        return merge(found) if found else None
+
+    def row_merge(r, b_from, b_to, more):
+        found = []
+        for b in range(b_from, b_to):
+            for g in range(group0[b + 1], group0[b + 1] + -(-counts[b + 1] // per_line)):
+                if all(plan[b][t][0] != r for t in range(counts[b + 1]) if t // per_line == g - group0[b + 1]):
+                    continue
+                line = jnp.broadcast_to(row_stat[pl.ds(g, 1), :], (BPD, BLK))
+                key = jnp.broadcast_to(keys[pl.ds(g, 1), :], (BPD, BLK))
+                found.append(jnp.where(key == block_id + BPD * r, line, NEG))
+        if not found:
+            return merge(more) if more else None
+        top = over_lanes(functools.reduce(jnp.maximum, found), jnp.maximum)
+        total = functools.reduce(jnp.add, [jnp.exp(v - top) for v in found])
+        return merge(list(more) + [top + jnp.log(over_lanes(total, jnp.add))])
+
+    for b in tail:
+        if b == half:
+            for axis, combine in ((1, col_merge), (0, row_merge)):
+                for r in range(side):
+                    early = combine(r, 0, half - 1, [])
+                    if early is not None:
+                        stat_send[axis, r] = early
+        reduce_rows(b)
+        if b == half:
+            for late in reversed(tail):
+                spread_rows(late)
+        row_partials(b)
 
     def exchange(step, axis, source, slots):
         return [
@@ -352,26 +381,16 @@
             for r in range(1, side)
         ]
 
-    for r in range(side):
-        found = []
-        for o in range(side):
-            if (r, o) == (0, 0):
-                continue
-            p = pos[(o, r)]
-            line = jnp.broadcast_to(col_stat[pl.ds(p, 1), :], (BPD, BLK))
-            found.append(jnp.where(block_id == tab[p, 1], line, NEG))
-        stat_send[1, r] = merge(found)
-    exchanged = exchange(0, 1, lambda r: stat_send.at[1, r], stat_recv)
-    for r in range(side):
-        found = []
-        for g in range(group0[-1]):
-            line = jnp.broadcast_to(row_stat[pl.ds(g, 1), :], (BPD, BLK))
-            key = jnp.broadcast_to(keys[pl.ds(g, 1), :], (BPD, BLK))
-            found.append(jnp.where(key == block_id + BPD * r, line, NEG))
-        top = over_lanes(functools.reduce(jnp.maximum, found), jnp.maximum)
-        total = functools.reduce(jnp.add, [jnp.exp(v - top) for v in found])
-        stat_send[0, r] = top + jnp.log(over_lanes(total, jnp.add))
-    exchanged += exchange(0, 0, lambda r: stat_send.at[0, r], stat_recv)
+    def has_early(axis, r):
+        mine = [pos[slot] for slot in pos if slot[1 if axis == 1 else 0] == r]
+        return any(p < base[half - 1] for p in mine)
+
+    exchanged = []
+    for axis, combine in ((1, col_merge), (0, row_merge)):
+        for r in range(side):
+            early = [stat_send[axis, r]] if has_early(axis, r) else []
+            stat_send[axis, r] = combine(r, half - 1, half, early)
+        exchanged += exchange(0, axis, lambda r, axis=axis: stat_send.at[axis, r], stat_recv)
     for copy in exchanged:
         copy.wait_recv()
     dp_stat[0, 0] = merge([stat_send[0, 0]] + [stat_recv[0, r] for r in range(1, side)])
@@ -403,17 +422,16 @@
     level[1, 0] = lse_own
     exchanged = exchange(1, 0, lambda r: level.at[0, 0], level)
     exchanged += exchange(1, 1, lambda r: level.at[1, 0], level)
-    for stage in (stage4, stage5):
-        for b in reversed(tail):
-            stage(b)
+    stage4(half)
     for copy in exchanged:
         copy.wait_recv()
+    stage5(half)
 
     def two_sided(values, li, lj):
         li = jnp.broadcast_to(li, (BLK, BLK)).T
         return jnp.exp(values - li) + jnp.exp(values - lj)
 
-    def weights(b):
+    def weights(b, start=0, stop=None):
         def body(t, carry):
             p = base[b - 1] + t
             first, second = tab[p, 0], tab[p, 1]
@@ -424,7 +442,7 @@
             wt_ref[p] = w.T.astype(BF16)
             return carry
 
-        lax.fori_loop(0, counts[b], body, 0)
+        lax.fori_loop(start, counts[b] if stop is None else stop, body, 0)
 
     def contribution(axis, rel, c):
         slots = [o for o in range(side) if (rel, o) != (0, 0)]
@@ -446,23 +464,35 @@
             out[offset + k] = values[:, k * BLK : (k + 1) * BLK]
 
     scatters = [[None] * events for _ in flows]
+
+    def scatter_send(f, e, out):
+        axis, sign = flows[f]
+        scatters[f][e] = send(
+            out, ring_in[f][e], rs_send.at[f, e], rs_recv.at[f, e], ahead[axis](sign % side)
+        )
+
     for e in range(events):
         rho = half - (e + 1) // 2
-        if e == 0 or e % 2 == 1:
+        if e % 2 == 1:
+            if rho == half - 1:
+                stage4(rho)
+                stage5(rho)
             weights(rho)
         for f, (axis, sign) in enumerate(flows):
-            by_block(temp.at[f], 0, contribution(axis, (rho * sign) % side, chunk_of(sign, e)))
-        for f, (axis, sign) in enumerate(flows):
+            if e == 0 and sign > 0:
+                weights(half, side * axis, side if axis == 0 else None)
+            own_part = contribution(axis, (rho * sign) % side, chunk_of(sign, e))
             if e < 2:
-                out = fresh.at[f, e]
-                out[...] = temp[f].astype(BF16)
+                by_block(fresh.at[f, e], 0, own_part.astype(BF16))
+                scatter_send(f, e, fresh.at[f, e])
             else:
+                by_block(temp.at[f], 0, own_part)
+        if e >= 2:
+            for f in range(4):
                 scatters[f][e - 2].wait_recv()
                 out = ring_in[f][e - 2]
                 out[...] = (temp[f] + out[...].astype(F32)).astype(BF16)
-            scatters[f][e] = send(
-                out, ring_in[f][e], rs_send.at[f, e], rs_recv.at[f, e], ahead[axis](sign % side)
-            )
+                scatter_send(f, e, out)
 
     for k in range(BPD):
         line = lse_own[k : k + 1]
@@ -479,18 +509,29 @@
             by_block(temp.at[0], 0, contribution(axis, 0, c))
             acc[rows] = acc[rows] + temp[0]
     last = [e for e in range(events) if half - (e + 1) // 2 == 1]
-    for e in last:
+    for e in last[:-1]:
         for f, (axis, sign) in enumerate(flows):
             scatters[f][e].wait_recv()
             rows = pl.ds(chunk_of(sign, e) * HALF_BPD, HALF_BPD)
             acc[rows] = acc[rows] + ring_in[f][e][...].astype(F32)
     stores = []
-    for k in range(BPD):
-        done[k] = acc[k].astype(BF16)
-        stores.append(
-            pltpu.make_async_copy(done.at[k], grad_out.at[:, pl.ds(k * BLK, BLK)], out_sem.at[k])
-        )
-        stores[k].start()
+    e = last[-1]
+    for sign in (1, -1):
+        pair = [f for f in range(4) if flows[f][1] == sign]
+        for f in pair:
+            scatters[f][e].wait_recv()
+        for i in range(HALF_BPD):
+            k = chunk_of(sign, e) * HALF_BPD + i
+            total = acc[k]
+            for f in pair:
+                total = total + ring_in[f][e][i].astype(F32)
+            done[k] = total.astype(BF16)
+            stores.append(
+                pltpu.make_async_copy(
+                    done.at[k], grad_out.at[:, pl.ds(k * BLK, BLK)], out_sem.at[k]
+                )
+            )
+            stores[-1].start()
     for copy in stores:
         copy.wait()
     for copy in started:

time: 204 us -> 204 us (level)
  no operation moved by 1% of the time
where the time goes in v4:
time: 204 us
  Pallas kernels  199 us (98%)
  local copies, waits for them, and re-layouts  3.42 us (2%)
    pallas_call x1, Pallas kernels, fused(): pl.pallas_call(functools.partial(kernel, side, xs, 2.0 / math.sqrt(D)), o...  199 us

profile of v4, /device:TPU:1, one launch (start us, length us, event | category | flops | bytes accessed | tf_op | source)
XLA Modules:
  0.0 204.0 jit_solution(12488331768743230504)
XLA Ops:
  0.6 1.3 fusion.1.refs_2_
  1.9 198.6 %shard_map.59 = (f32[8,128]{1,0:T(8,128)}, bf16[448,1024]{1,0:T(8,128)(2,1)}) custom-call(bf16[448,1024]{1,0:T(8,128)(2,1)} %bitcast.8, s32[2,3072]{1,0:T(2,128)} %bitcast.9, s32[8,128]{1,0:T(8,128)} %fusion.1.refs_2_, s32[64,128]{1,0:T(8,128)} %constant.17.clone.refs_3_), custom_call_target="tpu_custom_call" | custom-call | flops 16192110592 | bytes 1835008 | tf_op jit(solution)/shard_map/pallas_call | solution.py:580
  200.6 0.0 copy-start
  200.6 0.7 copy-done
  201.2 0.6 copy.8
  201.8 2.2 %copy.9 = bf16[1024,448]{0,1:T(8,128)(2,1)} copy(bf16[1024,448]{0,1:T(8,128)(2,1)} %bitcast.6) | data formatting | bytes 1835008
Async XLA Ops:
  200.6 0.7 copy-start

commit v5 on v4

--- a/solution.py
+++ b/solution.py
@@ -365,8 +365,7 @@
                         stat_send[axis, r] = early
         reduce_rows(b)
         if b == half:
-            for late in reversed(tail):
-                spread_rows(late)
+            spread_rows(b)
         row_partials(b)
 
     def exchange(step, axis, source, slots):
@@ -407,6 +406,8 @@
         )
         for r in range(1, 2 * xs)
     ]
+    for b in tail[:-1]:
+        spread_rows(b)
     for copy in exchanged:
         copy.wait_recv()
     lane_group = lax.broadcasted_iota(jnp.int32, (BPD, BLK), 1) // rows_x

time: 204 us -> 198 us (0.971)
  Pallas kernels: 199 us -> 191 us
    pallas_call x1, Pallas kernels: 199 us -> 191 us  [fused(): pl.pallas_call(functools.partial(kernel, side, xs, 2.0 / math.sqrt(D)), o...]
where the time goes in v5:
time: 198 us; the launch traced here: 196 us
  Pallas kernels  191 us (96%)
  local copies, waits for them, and re-layouts  3.42 us (2%)
    pallas_call x1, Pallas kernels, fused(): pl.pallas_call(functools.partial(kernel, side, xs, 2.0 / math.sqrt(D)), o...  191 us

profile of v5, /device:TPU:1, one launch (start us, length us, event | category | flops | bytes accessed | tf_op | source)
XLA Modules:
  0.0 196.2 jit_solution(1674521639763695845)
XLA Ops:
  0.6 1.3 fusion.1.refs_2_
  1.9 190.9 %shard_map.59 = (f32[8,128]{1,0:T(8,128)}, bf16[448,1024]{1,0:T(8,128)(2,1)}) custom-call(bf16[448,1024]{1,0:T(8,128)(2,1)} %bitcast.8, s32[2,3072]{1,0:T(2,128)} %bitcast.9, s32[8,128]{1,0:T(8,128)} %fusion.1.refs_2_, s32[64,128]{1,0:T(8,128)} %constant.17.clone.refs_3_), custom_call_target="tpu_custom_call" | custom-call | flops 16192110592 | bytes 1835008 | tf_op jit(solution)/shard_map/pallas_call | solution.py:581
  192.8 0.0 copy-start
  192.8 0.7 copy-done
  193.5 0.6 copy.8
  194.1 2.2 %copy.9 = bf16[1024,448]{0,1:T(8,128)(2,1)} copy(bf16[1024,448]{0,1:T(8,128)(2,1)} %bitcast.6) | data formatting | bytes 1835008
Async XLA Ops:
  192.8 0.7 copy-start

commit v6 on v5

--- a/solution.py
+++ b/solution.py
@@ -439,11 +439,17 @@
             li = level[0, tab[p, 2], pl.ds(jnp.maximum(first, 0), 1), :]
             lj = level[1, tab[p, 3], pl.ds(jnp.maximum(second, 0), 1), :]
             w = jnp.where(first >= 0, two_sided(tile(b, t), li, lj), 0.0)
-            w_ref[p] = w.astype(BF16)
-            wt_ref[p] = w.T.astype(BF16)
+            w = w.astype(BF16)
+            w_ref[p] = w
+            wt_ref[p] = w.T
             return carry
 
-        lax.fori_loop(start, counts[b] if stop is None else stop, body, 0)
+        stop = counts[b] if stop is None else stop
+        if b == half:
+            for t in range(start, stop):
+                body(t, 0)
+        else:
+            lax.fori_loop(start, stop, body, 0)
 
     def contribution(axis, rel, c):
         slots = [o for o in range(side) if (rel, o) != (0, 0)]

time: 198 us -> 195 us (0.985)
  Pallas kernels: 191 us -> 189 us
    pallas_call x1, Pallas kernels: 191 us -> 189 us  [fused(): pl.pallas_call(functools.partial(kernel, side, xs, 2.0 / math.sqrt(D)), o...]
where the time goes in v6:
time: 195 us; the launch traced here: 194 us
  Pallas kernels  189 us (97%)
  local copies, waits for them, and re-layouts  3.42 us (2%)
    pallas_call x1, Pallas kernels, fused(): pl.pallas_call(functools.partial(kernel, side, xs, 2.0 / math.sqrt(D)), o...  189 us

profile of v6, /device:TPU:1, one launch (start us, length us, event | category | flops | bytes accessed | tf_op | source)
XLA Modules:
  0.0 194.0 jit_solution(8919719545468678065)
XLA Ops:
  0.6 1.3 fusion.1.refs_2_
  1.9 188.6 %shard_map.59 = (f32[8,128]{1,0:T(8,128)}, bf16[448,1024]{1,0:T(8,128)(2,1)}) custom-call(bf16[448,1024]{1,0:T(8,128)(2,1)} %bitcast.8, s32[2,3072]{1,0:T(2,128)} %bitcast.9, s32[8,128]{1,0:T(8,128)} %fusion.1.refs_2_, s32[64,128]{1,0:T(8,128)} %constant.17.clone.refs_3_), custom_call_target="tpu_custom_call" | custom-call | flops 16192110592 | bytes 1835008 | tf_op jit(solution)/shard_map/pallas_call | solution.py:587
  190.5 0.0 copy-start
  190.6 0.7 copy-done
  191.2 0.6 copy.8
  191.8 2.2 %copy.9 = bf16[1024,448]{0,1:T(8,128)(2,1)} copy(bf16[1024,448]{0,1:T(8,128)(2,1)} %bitcast.6) | data formatting | bytes 1835008
Async XLA Ops:
  190.5 0.7 copy-start
